TPU v7x, 256 devices: a whole 4x4x8 slice. The times are simulated.
256 devices in a mesh: gz: 4 (over y), xy: 64 (over z, x, core).
Axes of the slice: x: 4, y: 4, z: 8, core: 2. Of those that a mesh axis runs over, the one named last changes fastest.
Arguments:
- sections: bfloat16 [4, 8192, 1024], P('gz', 'xy'), may hold values from -6 to 6
- peak_offsets: int32 [2, 4, 64, 8], P(None, 'gz', 'xy'), may hold values from -2 to 2
- confidence: int32 [4, 64, 8], P('gz', 'xy'), may hold values from 1 to 4
- tissue_mask: int32 [4, 64, 8], P('gz', 'xy'), may hold values 0 or 1
Outputs:
- flow_field: float32 [2, 4, 64, 8], P(None, 'gz', 'xy')
- correction: float32 [2, 4, 64, 8], P(None, 'gz', 'xy')
All inputs are finite; a program needn't handle non-finite values. No bound on the sum of `tissue_mask` on one device may be relied on, other than what follows from the above.
Results may differ from a plain program's by a relative error of at most 0.0003.
Values may be sent and summed in bfloat16 or wider, within the bound.
No kernel may reach another device: no remote copies, remote signals or barrier semaphores. Data moves between devices by JAX's collectives and lax.ppermute only.
A program may use at most 128 MiB of HBM per device.

v0:
```python
import jax
import jax.numpy as jnp
from jax import lax
from jax.sharding import PartitionSpec as P

PATCH = 128
ITERS = 4


STEP_SIZE = 0.12


def from_behind(block, axis, distance):
    devices = range(lax.axis_size(axis))
    route = [(i - distance, i) for i in devices if i - distance in devices]
    return lax.ppermute(block, axis, route)


def prefix(part, axis, combine, identity):
    place = lax.axis_index(axis)
    gathered = lax.all_gather(part, axis)
    state = jnp.zeros_like(part) + jnp.asarray(identity, part.dtype)

    def one(step, state):
        return combine(state, lax.dynamic_index_in_dim(gathered, step, 0, False))

    return lax.fori_loop(0, place, one, state)


def padded_2(array, sides, width):
    for axis, dim in sides:
        count, length = (lax.axis_size(axis), array.shape[dim])
        up = [(i, (i + 1) % count) for i in range(count - 1)]
        down = [(j, i) for i, j in up]
        last = lax.slice_in_dim(array, length - width, length, axis=dim)
        first = lax.slice_in_dim(array, 0, width, axis=dim)
        before = lax.ppermute(last, axis, up)
        after = lax.ppermute(first, axis, down)
        array = jnp.concatenate([before, array, after], axis=dim)
    return array


def score_table(current, previous):
    rows = current.shape[0] // PATCH
    columns = current.shape[1] // PATCH
    moving = current.reshape(rows, PATCH, columns, PATCH)
    fixed_img = previous.reshape(rows, PATCH, columns, PATCH).astype(jnp.float32)
    tables = []
    for shift_y in range(-3, 4):
        rolled_y = jnp.roll(moving, -shift_y, axis=1)
        for shift_x in range(-3, 4):
            window = jnp.roll(rolled_y, -shift_x, axis=3).astype(jnp.float32)
            tables.append(jnp.sum(fixed_img * window, axis=(1, 3)) / PATCH)
    return jnp.stack(tables).reshape(7, 7, rows, columns)


def pick_score(table, want_y, want_x):
    levels = jnp.arange(7, dtype=jnp.int32) - 3
    hit_y = (levels[:, None, None] == want_y[None]).astype(jnp.float32)
    hit_x = (levels[:, None, None] == want_x[None]).astype(jnp.float32)
    return jnp.sum(table * hit_y[:, None] * hit_x[None], axis=(0, 1))


def correlate(current, previous, peak):
    table = score_table(current, previous)
    center = pick_score(table, peak[0], peak[1])
    y_plus = pick_score(table, peak[0] + 1, peak[1])
    y_minus = pick_score(table, peak[0] - 1, peak[1])
    x_plus = pick_score(table, peak[0], peak[1] + 1)
    x_minus = pick_score(table, peak[0], peak[1] - 1)
    delta_y = (y_plus - y_minus) / (jnp.abs(y_minus) + jnp.abs(center) + jnp.abs(y_plus) + 1.0)
    delta_x = (x_plus - x_minus) / (jnp.abs(x_minus) + jnp.abs(center) + jnp.abs(x_plus) + 1.0)
    return jnp.stack([delta_y, delta_x])


def correlate_many(currents, previous_set, peak_set):

    def one_pair(items):
        return correlate(items[0], items[1], items[2])

    return lax.map(one_pair, (currents, previous_set, peak_set))


def spring_force(
    nodes,
    below,
    above,
    rows_up,
    rows_down,
    has_up,
    has_down,
    stiffness,
    next_stiff,
    flow_field,
    next_flow,
):
    force = jnp.where(has_up[None, None, :, None], rows_up - nodes, 0.0)
    force = force + jnp.where(has_down[None, None, :, None], rows_down - nodes, 0.0)
    zero_col = jnp.zeros(nodes.shape[:3] + (1,), jnp.float32)
    force = force + jnp.concatenate([zero_col, nodes[..., :-1] - nodes[..., 1:]], axis=3)
    force = force + jnp.concatenate([nodes[..., 1:] - nodes[..., :-1], zero_col], axis=3)
    force = force + stiffness[None] * (below + flow_field - nodes)
    force = force + next_stiff[None] * (above - next_flow - nodes)
    return force


def on_device(sections, peak_offsets, confidence, tissue_mask):
    local_count = sections.shape[0]
    peak_major = jnp.transpose(peak_offsets, (1, 0, 2, 3))
    before = from_behind(sections, "gz", 1)
    previous_set = jnp.concatenate([before, sections[:-1]], axis=0)
    deltas = correlate_many(sections, previous_set, peak_major)
    flow_field = peak_offsets.astype(jnp.float32) + jnp.transpose(deltas, (1, 0, 2, 3))
    group = lax.axis_index("gz")
    strip = lax.axis_index("xy")
    order = group * local_count + jnp.arange(local_count, dtype=jnp.int32)
    stiffness = confidence.astype(jnp.float32) * 0.25 * tissue_mask.astype(jnp.float32)
    stiffness = stiffness * (order > 0).astype(jnp.float32)[:, None, None]
    totals = jnp.sum(flow_field, axis=1)
    offset = prefix(
        totals, "gz", lambda earlier, later_sum: earlier + later_sum, jnp.zeros_like(totals)
    )
    start = jnp.cumsum(flow_field, axis=1) + offset[:, None]
    strip_rows = peak_offsets.shape[2]
    flow_first, stiff_first = from_behind((flow_field, stiffness), "gz", -1)
    next_stiff = jnp.concatenate([stiffness[1:], stiff_first], axis=0)
    next_flow = jnp.concatenate([flow_field[:, 1:], flow_first], axis=1)
    row_ids = strip * strip_rows + jnp.arange(strip_rows, dtype=jnp.int32)
    has_up = row_ids > 0
    has_down = row_ids < strip_rows * lax.axis_size("xy") - 1
    nodes = start
    for iteration in range(ITERS):
        padded = padded_2(nodes, (("gz", 1), ("xy", 2)), 1)
        inner = padded[:, 1:-1]
        force = spring_force(
            nodes,
            padded[:, :-2, 1:-1],
            padded[:, 2:, 1:-1],
            inner[:, :, :-2],
            inner[:, :, 2:],
            has_up,
            has_down,
            stiffness,
            next_stiff,
            flow_field,
            next_flow,
        )
        nodes = nodes + STEP_SIZE * force
    return (flow_field, nodes - start)


def solution(mesh):
    in_specs = (
        P("gz", "xy", None),
        P(None, "gz", "xy", None),
        P("gz", "xy", None),
        P("gz", "xy", None),
    )
    out_specs = (P(None, "gz", "xy", None), P(None, "gz", "xy", None))
    return jax.shard_map(
        on_device, mesh=mesh, in_specs=in_specs, out_specs=out_specs, check_vma=False
    )
```

profile of v0, /device:TPU:103, one launch (start us, length us, event | category | flops | bytes accessed | tf_op | source)
XLA Modules:
  0.0 241.4 jit_solution(7477508218327268068)
XLA Ops:
  0.6 3.2 %collective-permute-start = (bf16[1,128,1024]{2,1,0:T(8,128)(2,1)}, bf16[1,128,1024]{2,1,0:T(8,128)(2,1)S(1)}, u32[]{:S(2)}, u32[]{:S(2)}) collective-permute-start(bf16[1,128,1024]{2,1,0:T(8,128)(2,1)} %param.6), channel_id=1, source_target_pairs={{0,64},{64,128},{128,192},{1,65},{65,129},{129,193},{2,66},{66,130... | collective-permute-start | bytes 786440 | tf_op jit(solution)/shard_map/ppermute | solution.py:16
  90.6 2.0 reshape.3632
  92.5 1.9 reshape.3633
  94.4 1.9 reshape.3636
  96.4 1.9 reshape.3629
  98.3 1.9 reshape.3635
  100.2 1.9 reshape.3634
  102.1 1.9 reshape.3628
  104.1 1.9 reshape.3664
  106.0 1.9 reshape.3623
  108.6 4.0 %fusion.46 = (f32[1024]{0:T(1024)S(1)}, f32[1024]{0:T(1024)S(1)}, f32[1024]{0:T(1024)S(1)}, f32[1024]{0:T(1024)S(1)}, f32[1024]{0:T(1024)S(1)}, /*index=5*/f32[1...) fusion(f32[1,128,1024]{2,1,0:T(8,128)} %reshape.3662, ...), kind=kLoop, calls=%fused_computation.162 | loop fusion | flops 5620736 | bytes 7401472 | tf_op jit(solution)/shard_map/while/body/eval_jaxpr/reduce_sum | solution.py:53
  115.7 4.5 %fusion.47 = (f32[1024]{0:T(1024)S(1)}, f32[1024]{0:T(1024)S(1)}, f32[1024]{0:T(1024)S(1)}, f32[1024]{0:T(1024)S(1)}, f32[1024]{0:T(1024)S(1)}, /*index=5*/f32[1...) fusion(f32[1,128,1024]{2,1,0:T(8,128)} %reshape.3663, ...), kind=kLoop, calls=%fused_computation.163 | loop fusion | flops 5225472 | bytes 8720384 | tf_op jit(solution)/shard_map/while/body/eval_jaxpr/reduce_sum | solution.py:53
  134.9 3.4 %fusion.48 = (f32[1024]{0:T(1024)S(1)}, f32[1024]{0:T(1024)S(1)}, f32[1024]{0:T(1024)S(1)}, f32[1024]{0:T(1024)S(1)}, f32[1024]{0:T(1024)S(1)}, /*index=5*/f32[1...) fusion(f32[1,128,1024]{2,1,0:T(8,128)} %reshape.3664, ...), kind=kLoop, calls=%fused_computation.164 | loop fusion | flops 5357568 | bytes 8192000 | tf_op jit(solution)/shard_map/while/body/eval_jaxpr/reduce_sum | solution.py:53
  145.4 9.3 %all-gather = f32[8,1,1,8]{3,2,1,0:T(1,128)S(1)} all-gather(f32[2,1,1,8]{3,2,1,0:T(1,128)S(1)} %bitcast.358), channel_id=2, replica_groups=mesh['gz'=4,'xy'=64] {'gz'}, dimensions={0}, use_global_device_ids=true | all-gather | bytes 320 | tf_op jit(solution)/shard_map/all_gather | solution.py:21
  158.7 1.6 collective-permute-done.2
  160.4 8.9 %collective-permute-start.3 = (f32[2,3,1,8]{3,0,2,1:T(2,128)S(1)}, f32[2,3,1,8]{3,0,2,1:T(2,128)S(1)}, u32[]{:S(2)}, u32[]{:S(2)}) collective-permute-start(f32[2,3,1,8]{3,0,2,1:T(2,128)S(1)} %pad_maximum_fusion.6), channel_id=1, source_target_pairs={{0,1},{1,2},{2,3},{3,4},{4,5},{5,6},{6,7},{7,8},{8,9},{9,10},{10,1... | collective-permute-start | bytes 584 | tf_op jit(solution)/shard_map/ppermute | solution.py:37
  169.3 1.9 collective-permute-start.4
  171.3 6.3 %collective-permute-done.4 = f32[2,3,1,8]{3,0,2,1:T(2,128)S(1)} collective-permute-done((f32[2,3,1,8]{3,0,2,1:T(2,128)S(1)}, f32[2,3,1,8]{3,0,2,1:T(2,128)S(1)}, u32[]{:S(2)}, u32[]{:S(2)}) %collective-permute-start.4) | collective-permute-done | bytes 224 | tf_op jit(solution)/shard_map/ppermute | solution.py:38
  178.3 3.1 %collective-permute-start.7 = (f32[2,1,1,8]{3,0,2,1:T(2,128)S(1)}, f32[2,1,1,8]{3,0,2,1:T(2,128)S(1)}, u32[]{:S(2)}, u32[]{:S(2)}) collective-permute-start(f32[2,1,1,8]{3,0,2,1:T(2,128)S(1)} %multiply_add_fusion.2), channel_id=1, source_target_pairs={{0,64},{64,128},{128,192},{1,65},{65,129},{129,193},{2,66},{66,130... | collective-permute-start | bytes 200 | tf_op jit(solution)/shard_map/ppermute | solution.py:37
  182.7 3.0 %collective-permute-done.8 = f32[2,1,1,8]{3,0,2,1:T(2,128)S(1)} collective-permute-done((f32[2,1,1,8]{3,0,2,1:T(2,128)S(1)}, f32[2,1,1,8]{3,0,2,1:T(2,128)S(1)}, u32[]{:S(2)}, u32[]{:S(2)}) %collective-permute-start.8) | collective-permute-done | bytes 96 | tf_op jit(solution)/shard_map/ppermute | solution.py:38
  185.7 1.9 collective-permute-start.10
  187.7 7.0 %collective-permute-start.9 = (f32[2,3,1,8]{3,0,2,1:T(2,128)S(1)}, f32[2,3,1,8]{3,0,2,1:T(2,128)S(1)}, u32[]{:S(2)}, u32[]{:S(2)}) collective-permute-start(f32[2,3,1,8]{3,0,2,1:T(2,128)S(1)} %pad_maximum_fusion.7), channel_id=1, source_target_pairs={{0,1},{1,2},{2,3},{3,4},{4,5},{5,6},{6,7},{7,8},{8,9},{9,10},{10,1... | collective-permute-start | bytes 584 | tf_op jit(solution)/shard_map/ppermute | solution.py:37
  196.1 2.7 %collective-permute-start.11 = (f32[2,1,1,8]{3,0,2,1:T(2,128)S(1)}, f32[2,1,1,8]{3,0,2,1:T(2,128)S(1)}, u32[]{:S(2)}, u32[]{:S(2)}) collective-permute-start(f32[2,1,1,8]{3,0,2,1:T(2,128)S(1)} %multiply_add_fusion.1), channel_id=1, source_target_pairs={{0,64},{64,128},{128,192},{1,65},{65,129},{129,193},{2,66},{66,130... | collective-permute-start | bytes 200 | tf_op jit(solution)/shard_map/ppermute | solution.py:37
  200.1 3.0 %collective-permute-done.12 = f32[2,1,1,8]{3,0,2,1:T(2,128)S(1)} collective-permute-done((f32[2,1,1,8]{3,0,2,1:T(2,128)S(1)}, f32[2,1,1,8]{3,0,2,1:T(2,128)S(1)}, u32[]{:S(2)}, u32[]{:S(2)}) %collective-permute-start.12) | collective-permute-done | bytes 96 | tf_op jit(solution)/shard_map/ppermute | solution.py:38
  203.1 8.9 %collective-permute-start.13 = (f32[2,3,1,8]{3,0,2,1:T(2,128)S(1)}, f32[2,3,1,8]{3,0,2,1:T(2,128)S(1)}, u32[]{:S(2)}, u32[]{:S(2)}) collective-permute-start(f32[2,3,1,8]{3,0,2,1:T(2,128)S(1)} %pad_maximum_fusion.8), channel_id=1, source_target_pairs={{0,1},{1,2},{2,3},{3,4},{4,5},{5,6},{6,7},{7,8},{8,9},{9,10},{10,1... | collective-permute-start | bytes 584 | tf_op jit(solution)/shard_map/ppermute | solution.py:37
  212.0 1.9 collective-permute-start.14
  214.0 6.2 %collective-permute-done.14 = f32[2,3,1,8]{3,0,2,1:T(2,128)S(1)} collective-permute-done((f32[2,3,1,8]{3,0,2,1:T(2,128)S(1)}, f32[2,3,1,8]{3,0,2,1:T(2,128)S(1)}, u32[]{:S(2)}, u32[]{:S(2)}) %collective-permute-start.14) | collective-permute-done | bytes 224 | tf_op jit(solution)/shard_map/ppermute | solution.py:38
  221.0 3.1 %collective-permute-start.15 = (f32[2,1,1,8]{3,0,2,1:T(2,128)S(1)}, f32[2,1,1,8]{3,0,2,1:T(2,128)S(1)}, u32[]{:S(2)}, u32[]{:S(2)}) collective-permute-start(f32[2,1,1,8]{3,0,2,1:T(2,128)S(1)} %multiply_add_fusion), channel_id=1, source_target_pairs={{0,64},{64,128},{128,192},{1,65},{65,129},{129,193},{2,66},{66,130... | collective-permute-start | bytes 200 | tf_op jit(solution)/shard_map/ppermute | solution.py:37
  225.4 3.0 %collective-permute-done.16 = f32[2,1,1,8]{3,0,2,1:T(2,128)S(1)} collective-permute-done((f32[2,1,1,8]{3,0,2,1:T(2,128)S(1)}, f32[2,1,1,8]{3,0,2,1:T(2,128)S(1)}, u32[]{:S(2)}, u32[]{:S(2)}) %collective-permute-start.16) | collective-permute-done | bytes 96 | tf_op jit(solution)/shard_map/ppermute | solution.py:38
  228.4 3.4 %collective-permute-start.17 = (f32[2,3,1,8]{3,0,2,1:T(2,128)S(1)}, f32[2,3,1,8]{3,0,2,1:T(2,128)S(1)}, u32[]{:S(2)}, u32[]{:S(2)}) collective-permute-start(f32[2,3,1,8]{3,0,2,1:T(2,128)S(1)} %pad_maximum_fusion.9), channel_id=1, source_target_pairs={{0,1},{1,2},{2,3},{3,4},{4,5},{5,6},{6,7},{7,8},{8,9},{9,10},{10,1... | collective-permute-start | bytes 584 | tf_op jit(solution)/shard_map/ppermute | solution.py:37
  231.8 1.9 collective-permute-start.18
  233.8 6.2 %collective-permute-done.18 = f32[2,3,1,8]{3,0,2,1:T(2,128)S(1)} collective-permute-done((f32[2,3,1,8]{3,0,2,1:T(2,128)S(1)}, f32[2,3,1,8]{3,0,2,1:T(2,128)S(1)}, u32[]{:S(2)}, u32[]{:S(2)}) %collective-permute-start.18) | collective-permute-done | bytes 224 | tf_op jit(solution)/shard_map/ppermute | solution.py:38
  (418 shorter events, 123.9 us)
Async XLA Ops:
  0.6 108.0 %collective-permute-start = (bf16[1,128,1024]{2,1,0:T(8,128)(2,1)}, bf16[1,128,1024]{2,1,0:T(8,128)(2,1)S(1)}, u32[]{:S(2)}, u32[]{:S(2)}) collective-permute-start(bf16[1,128,1024]{2,1,0:T(8,128)(2,1)} %param.6), channel_id=1, source_target_pairs={{0,64},{64,128},{128,192},{1,65},{65,129},{129,193},{2,66},{66,130... | collective-permute-start | bytes 786440 | tf_op jit(solution)/shard_map/ppermute | solution.py:16
  5.1 166.2 %collective-permute-start.5 = (f32[1,1,8]{2,1,0:T(1,128)}, f32[1,1,8]{2,1,0:T(1,128)}, u32[]{:S(2)}, u32[]{:S(2)}) collective-permute-start(f32[1,1,8]{2,1,0:T(1,128)} %multiply_multiply_fusion), channel_id=1, source_target_pairs={{64,0},{128,64},{192,128},{65,1},{129,65},{193,129},{66,2},{130,66... | collective-permute-start | bytes 104 | tf_op jit(solution)/shard_map/ppermute | solution.py:16
  52.2 1.9 copy-start.1
  141.6 1.4 copy-start.34
  141.6 1.4 copy-start.35
  141.6 1.4 copy-start.36
  141.6 1.4 copy-start.37
  141.6 1.4 copy-start.38
  141.6 1.4 copy-start.39
  141.6 1.4 copy-start.40
  141.6 1.4 copy-start.41
  141.6 1.4 copy-start.42
  141.6 1.4 copy-start.43
  141.7 1.4 copy-start.44
  145.4 94.6 %copy-start.29 = (f32[2,1,1,8]{3,0,2,1:T(2,128)}, f32[2,1,1,8]{3,0,2,1:T(2,128)S(1)}, u32[]{:S(2)}) copy-start(f32[2,1,1,8]{3,0,2,1:T(2,128)S(1)} %convert_add_fusion) | copy-start | bytes 196
  154.8 4.0 %collective-permute-start.1 = (f32[2,1,1,8]{3,0,2,1:T(2,128)S(1)}, f32[2,1,1,8]{3,0,2,1:T(2,128)S(1)}, u32[]{:S(2)}, u32[]{:S(2)}) collective-permute-start(f32[2,1,1,8]{3,0,2,1:T(2,128)S(1)} %bitcast_add_fusion.1), channel_id=1, source_target_pairs={{0,64},{64,128},{128,192},{1,65},{65,129},{129,193},{2,66},{66,130... | collective-permute-start | bytes 200 | tf_op jit(solution)/shard_map/ppermute | solution.py:37
  156.0 4.3 %collective-permute-start.2 = (f32[2,1,1,8]{3,0,2,1:T(2,128)S(1)}, f32[2,1,1,8]{3,0,2,1:T(2,128)S(1)}, u32[]{:S(2)}, u32[]{:S(2)}) collective-permute-start(f32[2,1,1,8]{3,0,2,1:T(2,128)S(1)} %bitcast_add_fusion.1), channel_id=1, source_target_pairs={{64,0},{128,64},{192,128},{65,1},{129,65},{193,129},{66,2},{130,66... | collective-permute-start | bytes 200 | tf_op jit(solution)/shard_map/ppermute | solution.py:38
  157.4 13.8 %collective-permute-start.6 = (f32[2,1,1,8]{3,0,2,1:T(2,128)S(1)}, f32[2,1,1,8]{3,0,2,1:T(2,128)S(1)}, u32[]{:S(2)}, u32[]{:S(2)}) collective-permute-start(f32[2,1,1,8]{3,0,2,1:T(2,128)S(1)} %convert_add_fusion), channel_id=1, source_target_pairs={{64,0},{128,64},{192,128},{65,1},{129,65},{193,129},{66,2},{130,66... | collective-permute-start | bytes 200 | tf_op jit(solution)/shard_map/ppermute | solution.py:16
  160.4 10.9 %collective-permute-start.3 = (f32[2,3,1,8]{3,0,2,1:T(2,128)S(1)}, f32[2,3,1,8]{3,0,2,1:T(2,128)S(1)}, u32[]{:S(2)}, u32[]{:S(2)}) collective-permute-start(f32[2,3,1,8]{3,0,2,1:T(2,128)S(1)} %pad_maximum_fusion.6), channel_id=1, source_target_pairs={{0,1},{1,2},{2,3},{3,4},{4,5},{5,6},{6,7},{7,8},{8,9},{9,10},{10,1... | collective-permute-start | bytes 584 | tf_op jit(solution)/shard_map/ppermute | solution.py:37
  169.3 8.2 %collective-permute-start.4 = (f32[2,3,1,8]{3,0,2,1:T(2,128)S(1)}, f32[2,3,1,8]{3,0,2,1:T(2,128)S(1)}, u32[]{:S(2)}, u32[]{:S(2)}) collective-permute-start(f32[2,3,1,8]{3,0,2,1:T(2,128)S(1)} %pad_maximum_fusion.6), channel_id=1, source_target_pairs={{1,0},{2,1},{3,2},{4,3},{5,4},{6,5},{7,6},{8,7},{9,8},{10,9},{11,1... | collective-permute-start | bytes 584 | tf_op jit(solution)/shard_map/ppermute | solution.py:38
  178.3 4.4 %collective-permute-start.7 = (f32[2,1,1,8]{3,0,2,1:T(2,128)S(1)}, f32[2,1,1,8]{3,0,2,1:T(2,128)S(1)}, u32[]{:S(2)}, u32[]{:S(2)}) collective-permute-start(f32[2,1,1,8]{3,0,2,1:T(2,128)S(1)} %multiply_add_fusion.2), channel_id=1, source_target_pairs={{0,64},{64,128},{128,192},{1,65},{65,129},{129,193},{2,66},{66,130... | collective-permute-start | bytes 200 | tf_op jit(solution)/shard_map/ppermute | solution.py:37
  181.4 4.3 %collective-permute-start.8 = (f32[2,1,1,8]{3,0,2,1:T(2,128)S(1)}, f32[2,1,1,8]{3,0,2,1:T(2,128)S(1)}, u32[]{:S(2)}, u32[]{:S(2)}) collective-permute-start(f32[2,1,1,8]{3,0,2,1:T(2,128)S(1)} %multiply_add_fusion.2), channel_id=1, source_target_pairs={{64,0},{128,64},{192,128},{65,1},{129,65},{193,129},{66,2},{130,66... | collective-permute-start | bytes 200 | tf_op jit(solution)/shard_map/ppermute | solution.py:38
  185.7 9.0 %collective-permute-start.10 = (f32[2,3,1,8]{3,0,2,1:T(2,128)S(1)}, f32[2,3,1,8]{3,0,2,1:T(2,128)S(1)}, u32[]{:S(2)}, u32[]{:S(2)}) collective-permute-start(f32[2,3,1,8]{3,0,2,1:T(2,128)S(1)} %pad_maximum_fusion.7), channel_id=1, source_target_pairs={{1,0},{2,1},{3,2},{4,3},{5,4},{6,5},{7,6},{8,7},{9,8},{10,9},{11,1... | collective-permute-start | bytes 584 | tf_op jit(solution)/shard_map/ppermute | solution.py:38
  187.7 7.7 %collective-permute-start.9 = (f32[2,3,1,8]{3,0,2,1:T(2,128)S(1)}, f32[2,3,1,8]{3,0,2,1:T(2,128)S(1)}, u32[]{:S(2)}, u32[]{:S(2)}) collective-permute-start(f32[2,3,1,8]{3,0,2,1:T(2,128)S(1)} %pad_maximum_fusion.7), channel_id=1, source_target_pairs={{0,1},{1,2},{2,3},{3,4},{4,5},{5,6},{6,7},{7,8},{8,9},{9,10},{10,1... | collective-permute-start | bytes 584 | tf_op jit(solution)/shard_map/ppermute | solution.py:37
  196.1 4.0 %collective-permute-start.11 = (f32[2,1,1,8]{3,0,2,1:T(2,128)S(1)}, f32[2,1,1,8]{3,0,2,1:T(2,128)S(1)}, u32[]{:S(2)}, u32[]{:S(2)}) collective-permute-start(f32[2,1,1,8]{3,0,2,1:T(2,128)S(1)} %multiply_add_fusion.1), channel_id=1, source_target_pairs={{0,64},{64,128},{128,192},{1,65},{65,129},{129,193},{2,66},{66,130... | collective-permute-start | bytes 200 | tf_op jit(solution)/shard_map/ppermute | solution.py:37
  198.8 4.3 %collective-permute-start.12 = (f32[2,1,1,8]{3,0,2,1:T(2,128)S(1)}, f32[2,1,1,8]{3,0,2,1:T(2,128)S(1)}, u32[]{:S(2)}, u32[]{:S(2)}) collective-permute-start(f32[2,1,1,8]{3,0,2,1:T(2,128)S(1)} %multiply_add_fusion.1), channel_id=1, source_target_pairs={{64,0},{128,64},{192,128},{65,1},{129,65},{193,129},{66,2},{130,66... | collective-permute-start | bytes 200 | tf_op jit(solution)/shard_map/ppermute | solution.py:38
  203.1 10.9 %collective-permute-start.13 = (f32[2,3,1,8]{3,0,2,1:T(2,128)S(1)}, f32[2,3,1,8]{3,0,2,1:T(2,128)S(1)}, u32[]{:S(2)}, u32[]{:S(2)}) collective-permute-start(f32[2,3,1,8]{3,0,2,1:T(2,128)S(1)} %pad_maximum_fusion.8), channel_id=1, source_target_pairs={{0,1},{1,2},{2,3},{3,4},{4,5},{5,6},{6,7},{7,8},{8,9},{9,10},{10,1... | collective-permute-start | bytes 584 | tf_op jit(solution)/shard_map/ppermute | solution.py:37
  212.0 8.2 %collective-permute-start.14 = (f32[2,3,1,8]{3,0,2,1:T(2,128)S(1)}, f32[2,3,1,8]{3,0,2,1:T(2,128)S(1)}, u32[]{:S(2)}, u32[]{:S(2)}) collective-permute-start(f32[2,3,1,8]{3,0,2,1:T(2,128)S(1)} %pad_maximum_fusion.8), channel_id=1, source_target_pairs={{1,0},{2,1},{3,2},{4,3},{5,4},{6,5},{7,6},{8,7},{9,8},{10,9},{11,1... | collective-permute-start | bytes 584 | tf_op jit(solution)/shard_map/ppermute | solution.py:38
  221.0 4.4 %collective-permute-start.15 = (f32[2,1,1,8]{3,0,2,1:T(2,128)S(1)}, f32[2,1,1,8]{3,0,2,1:T(2,128)S(1)}, u32[]{:S(2)}, u32[]{:S(2)}) collective-permute-start(f32[2,1,1,8]{3,0,2,1:T(2,128)S(1)} %multiply_add_fusion), channel_id=1, source_target_pairs={{0,64},{64,128},{128,192},{1,65},{65,129},{129,193},{2,66},{66,130... | collective-permute-start | bytes 200 | tf_op jit(solution)/shard_map/ppermute | solution.py:37
  224.1 4.3 %collective-permute-start.16 = (f32[2,1,1,8]{3,0,2,1:T(2,128)S(1)}, f32[2,1,1,8]{3,0,2,1:T(2,128)S(1)}, u32[]{:S(2)}, u32[]{:S(2)}) collective-permute-start(f32[2,1,1,8]{3,0,2,1:T(2,128)S(1)} %multiply_add_fusion), channel_id=1, source_target_pairs={{64,0},{128,64},{192,128},{65,1},{129,65},{193,129},{66,2},{130,66... | collective-permute-start | bytes 200 | tf_op jit(solution)/shard_map/ppermute | solution.py:38
  228.4 5.4 %collective-permute-start.17 = (f32[2,3,1,8]{3,0,2,1:T(2,128)S(1)}, f32[2,3,1,8]{3,0,2,1:T(2,128)S(1)}, u32[]{:S(2)}, u32[]{:S(2)}) collective-permute-start(f32[2,3,1,8]{3,0,2,1:T(2,128)S(1)} %pad_maximum_fusion.9), channel_id=1, source_target_pairs={{0,1},{1,2},{2,3},{3,4},{4,5},{5,6},{6,7},{7,8},{8,9},{9,10},{10,1... | collective-permute-start | bytes 584 | tf_op jit(solution)/shard_map/ppermute | solution.py:37
  231.8 8.2 %collective-permute-start.18 = (f32[2,3,1,8]{3,0,2,1:T(2,128)S(1)}, f32[2,3,1,8]{3,0,2,1:T(2,128)S(1)}, u32[]{:S(2)}, u32[]{:S(2)}) collective-permute-start(f32[2,3,1,8]{3,0,2,1:T(2,128)S(1)} %pad_maximum_fusion.9), channel_id=1, source_target_pairs={{1,0},{2,1},{3,2},{4,3},{5,4},{6,5},{7,6},{8,7},{9,8},{10,9},{11,1... | collective-permute-start | bytes 584 | tf_op jit(solution)/shard_map/ppermute | solution.py:38
  (42 other events, 43.6 us)
where the time goes:
time: 244 us; the launch traced here: 241 us
  local copies, waits for them, and re-layouts  78.6 us (32%)
  other arithmetic  64.9 us (27%)
  starting transfers between devices  56.9 us (23%)
  waiting for transfers between devices  30.1 us (12%)
  blocking collectives  9.3 us (4%)
    convert_element_type x42, local copies, waits for them, and re-layouts, score_table(): window = jnp.roll(rolled_y, -shift_x, axis=3).astype(jnp.float32)  42.9 us
    ppermute x8, starting transfers between devices, padded_2(): before = lax.ppermute(last, axis, up)  38.3 us
    convert_element_type x39, other arithmetic, score_table(): window = jnp.roll(rolled_y, -shift_x, axis=3).astype(jnp.float32)  35.5 us
    ppermute x8, waiting for transfers between devices, padded_2(): after = lax.ppermute(first, axis, down)  29.4 us
    reduce_sum x53, other arithmetic, score_table(): tables.append(jnp.sum(fixed_img * window, axis=(1, 3)) / PATCH)  18.5 us
    unnamed x111, local copies, waits for them, and re-layouts  14.9 us
    another operation x51, local copies, waits for them, and re-layouts, score_table(): return jnp.stack(tables).reshape(7, 7, rows, columns)  14.4 us
    ppermute x8, starting transfers between devices, padded_2(): after = lax.ppermute(first, axis, down)  12.8 us
  transfers between devices with their start and end apart: 19, of which 8 were waited for; matrix products, arithmetic and copies ran while one was open for 52% of the time, Pallas kernels for 0%

commit v1 on v0

v1 whole, which is shorter than its diff:
```python
import jax
import jax.numpy as jnp
from jax import lax
from jax.experimental import pallas as pl
from jax.experimental.pallas import tpu as pltpu
from jax.sharding import PartitionSpec as P

PATCH = 128
LANES = 128
COLS = 8
ITERS = 4
STEP_SIZE = 0.12
PLANE = 8


def place():
    gz = lax.axis_index("gz")
    xy = lax.axis_index("xy")
    return gz, xy


def correlate_kernel(pk_ref, own_ref, got_ref, peak_ref, conf_ref, mask_ref, out_ref, pad_ref):
    gz, xy = place()
    odd = lax.rem(xy, 2)
    sign = 1 - 2 * odd
    target = gz + odd
    sums = []
    for j in range(COLS):
        cols = slice(j * PATCH, (j + 1) * PATCH)
        own = own_ref[0, :, cols].astype(jnp.float32)
        got = got_ref[0, :, cols].astype(jnp.float32)
        shift_y = -sign * pk_ref[0, 0, 0, j]
        shift_x = -sign * pk_ref[1, 0, 0, j]
        moved = pltpu.roll(own, lax.rem(shift_x + PATCH, PATCH), 1)
        pad_ref[j, 8 : 8 + PATCH, :] = moved
        pad_ref[j, 0:8, :] = moved[PATCH - 8 :, :]
        pad_ref[j, 8 + PATCH :, :] = moved[0:8, :]
        center = pad_ref[j, pl.ds(8 - shift_y, PATCH), :]
        windows = (
            center,
            pad_ref[j, pl.ds(9 - shift_y, PATCH), :],
            pad_ref[j, pl.ds(7 - shift_y, PATCH), :],
            pltpu.roll(center, PATCH - 1, 1),
            pltpu.roll(center, 1, 1),
        )
        sums.append(
            [
                jnp.sum(jnp.sum((w * got).reshape(PATCH // 8, 8, LANES), axis=0), axis=0, keepdims=True)
                for w in windows
            ]
        )
    scores = []
    for k in range(5):
        stacked = jnp.concatenate([sums[j][k] for j in range(COLS)], axis=0)
        scores.append(jnp.sum(stacked, axis=1, keepdims=True) * (1.0 / PATCH))
    center, y_plus, y_minus, x_plus, x_minus = scores
    paired = jnp.logical_and(target > 0, target < 4)
    scale = jnp.where(paired, sign, 0).astype(jnp.float32)
    delta_y = scale * (y_plus - y_minus) / (jnp.abs(y_minus) + jnp.abs(center) + jnp.abs(y_plus) + 1.0)
    delta_x = scale * (x_plus - x_minus) / (jnp.abs(x_minus) + jnp.abs(center) + jnp.abs(x_plus) + 1.0)
    lane = lax.broadcasted_iota(jnp.int32, (COLS, LANES), 1)
    patch = lax.broadcasted_iota(jnp.int32, (COLS, LANES), 0)
    spread = jnp.where(lane == target * 16 + patch, delta_y, 0.0)
    spread = spread + jnp.where(lane == target * 16 + COLS + patch, delta_x, 0.0)
    row = jnp.sum(spread, axis=0, keepdims=True)
    stiff = conf_ref[0].astype(jnp.float32) * 0.25 * mask_ref[0].astype(jnp.float32)
    stiff = stiff * (gz > 0).astype(jnp.float32)
    gap = jnp.zeros((1, 48), jnp.float32)
    fixed = jnp.concatenate(
        [
            peak_ref[0, 0].astype(jnp.float32),
            peak_ref[1, 0].astype(jnp.float32),
            gap,
            stiff,
            stiff,
            gap,
        ],
        axis=1,
    )
    row = row + pltpu.roll(fixed, gz * 16, 1)
    out_ref[...] = jnp.broadcast_to(row[None], out_ref.shape)


def relax_kernel(own_ref, got_ref, flow_ref, corr_ref):
    gz, xy = place()
    z = xy // PLANE
    inner = lax.rem(xy, PLANE)
    upper = inner < PLANE // 2

    def folded(ref):
        parts = [ref[g * PLANE : (g + 1) * PLANE, 0, :] for g in range(4)]
        return (parts[0] + parts[1]) + (parts[2] + parts[3])

    own = folded(own_ref)
    got = folded(got_ref)
    window = jnp.concatenate([jnp.where(upper, got, own), jnp.where(upper, own, got)], axis=0)
    base = jnp.where(upper, z - 1, z) * PLANE
    here = jnp.where(upper, PLANE + inner, inner)
    shape = (2 * PLANE, LANES)
    lane = lax.broadcasted_iota(jnp.int32, shape, 1)
    local = lax.broadcasted_iota(jnp.int32, shape, 0)
    row = local + base
    col = lax.rem(lane, COLS)
    has_up = row > 0
    has_down = row < 63
    has_left = col > 0
    has_right = col < COLS - 1
    flow = jnp.where(lane < 64, window, 0.0)
    stiff = jnp.where(lane < 64, pltpu.roll(window, 64, 1), 0.0)
    next_stiff = jnp.where(lane < 48, pltpu.roll(stiff, LANES - 16, 1), 0.0)
    next_flow = jnp.where(lane < 48, pltpu.roll(flow, LANES - 16, 1), 0.0)
    start = flow + jnp.where(lane >= 16, pltpu.roll(flow, 16, 1), 0.0)
    start = start + jnp.where(lane >= 32, pltpu.roll(start, 32, 1), 0.0)
    nodes = start
    for _ in range(ITERS):
        force = jnp.where(has_up, pltpu.roll(nodes, 1, 0) - nodes, 0.0)
        force = force + jnp.where(has_down, pltpu.roll(nodes, 2 * PLANE - 1, 0) - nodes, 0.0)
        force = force + jnp.where(has_left, pltpu.roll(nodes, 1, 1) - nodes, 0.0)
        force = force + jnp.where(has_right, pltpu.roll(nodes, LANES - 1, 1) - nodes, 0.0)
        force = force + stiff * (pltpu.roll(nodes, 16, 1) + flow - nodes)
        force = force + next_stiff * (pltpu.roll(nodes, LANES - 16, 1) - next_flow - nodes)
        nodes = nodes + STEP_SIZE * force
    turn = lax.rem(LANES - gz * 16, LANES)
    for value, ref in ((flow, flow_ref), (nodes - start, corr_ref)):
        mine = jnp.sum(jnp.where(local == here, value, 0.0), axis=0, keepdims=True)
        mine = pltpu.roll(mine, turn, 1)
        ref[0, 0] = mine[:, 0:COLS]
        ref[1, 0] = mine[:, COLS : 2 * COLS]


def on_device(sections, peak_offsets, confidence, tissue_mask):
    groups = lax.axis_size("gz")
    strips = lax.axis_size("xy")
    swap = []
    fetch = []
    for strip in range(strips):
        for group in range(groups):
            this = group * strips + strip
            after = (group + 1) % groups * strips + strip
            swap.append((this, after) if strip % 2 == 0 else (after, this))
            fetch.append((this, this) if strip % 2 == 0 else (after, this))
    got = lax.ppermute(sections, ("gz", "xy"), swap)
    peaks = lax.ppermute(peak_offsets, ("gz", "xy"), fetch)
    vmem = pl.BlockSpec(memory_space=pltpu.VMEM)
    smem = pl.BlockSpec(memory_space=pltpu.SMEM)
    row = pl.pallas_call(
        correlate_kernel,
        out_shape=jax.ShapeDtypeStruct((32, 1, LANES), jnp.float32),
        in_specs=[smem, vmem, vmem, vmem, vmem, vmem],
        out_specs=vmem,
        scratch_shapes=[pltpu.VMEM((COLS, PATCH + 16, LANES), jnp.float32)],
    )(peaks, sections, got, peak_offsets, confidence, tissue_mask)
    planes = [
        [group * strips + plane * PLANE + inner for group in range(groups) for inner in range(PLANE)]
        for plane in range(strips // PLANE)
    ]
    block = lax.all_to_all(row, ("gz", "xy"), 0, 0, axis_index_groups=planes, tiled=True)
    hop = []
    for device in range(groups * strips):
        group, strip = divmod(device, strips)
        step = PLANE if strip % PLANE < PLANE // 2 else -PLANE
        hop.append((device, group * strips + (strip + step) % strips))
    beside = lax.ppermute(block, ("gz", "xy"), hop)
    shape = jax.ShapeDtypeStruct(peak_offsets.shape, jnp.float32)
    return pl.pallas_call(
        relax_kernel,
        out_shape=(shape, shape),
        in_specs=[vmem, vmem],
        out_specs=(vmem, vmem),
    )(block, beside)


def solution(mesh):
    in_specs = (
        P("gz", "xy", None),
        P(None, "gz", "xy", None),
        P("gz", "xy", None),
        P("gz", "xy", None),
    )
    out_specs = (P(None, "gz", "xy", None), P(None, "gz", "xy", None))
    return jax.shard_map(
        on_device, mesh=mesh, in_specs=in_specs, out_specs=out_specs, check_vma=False
    )
```

time: 244 us -> 35.5 us (0.15)
  the two profiles are of different devices: /device:TPU:103 before, /device:TPU:1 now
where the time goes in v1:
time: 35.5 us; the launch traced here: 35.3 us
  blocking collectives  13.2 us (37%)
  starting transfers between devices  7.64 us (22%)
  waiting for transfers between devices  7.51 us (21%)
  Pallas kernels  4.43 us (12%)
  local copies, waits for them, and re-layouts  1.86 us (5%)
  between operations  0.65 us (2%)
    all_to_all x1, blocking collectives, on_device(): lax.all_to_all(row, ('gz', 'xy'), 0, 0, axis_index_groups=planes, tiled=T...  13.2 us
    ppermute x1, waiting for transfers between devices, on_device(): beside = lax.ppermute(block, ('gz', 'xy'), hop)  5.07 us
    ppermute x1, starting transfers between devices, on_device(): got = lax.ppermute(sections, ('gz', 'xy'), swap)  3.64 us
    pallas_call x1, Pallas kernels, on_device(): pl.pallas_call(correlate_kernel, out_shape=jax.ShapeDtypeStruct((32, 1, L...  2.51 us
    ppermute x1, waiting for transfers between devices, on_device(): peaks = lax.ppermute(peak_offsets, ('gz', 'xy'), fetch)  2.44 us
    ppermute x1, starting transfers between devices, on_device(): peaks = lax.ppermute(peak_offsets, ('gz', 'xy'), fetch)  2.36 us
    pallas_call x1, Pallas kernels, on_device(): pl.pallas_call(relax_kernel, out_shape=(shape, shape), in_specs=[vmem, vm...  1.92 us
    unnamed x8, local copies, waits for them, and re-layouts  1.86 us
  transfers between devices with their start and end apart: 3, of which 2 were waited for; matrix products, arithmetic and copies ran while one was open for 0% of the time, Pallas kernels for 0%

profile of v1, /device:TPU:1, one launch (start us, length us, event | category | flops | bytes accessed | tf_op | source)
XLA Modules:
  0.0 35.3 jit_solution(6177126677415154805)
XLA Ops:
  0.6 3.6 %collective-permute-start.1 = (bf16[1,128,1024]{2,1,0:T(8,128)(2,1)}, bf16[1,128,1024]{2,1,0:T(8,128)(2,1)S(1)}, u32[]{:S(2)}, u32[]{:S(2)}) collective-permute-start(bf16[1,128,1024]{2,1,0:T(8,128)(2,1)} %own_ref.1), channel_id=1, source_target_pairs={{0,64},{64,128},{128,192},{192,0},{65,1},{129,65},{193,129},{1,193... | collective-permute-start | bytes 786440 | tf_op jit(solution)/shard_map/ppermute | solution.py:142
  4.3 2.4 %collective-permute-start = (s32[2,1,1,8]{3,2,1,0:T(1,128)}, s32[2,1,1,8]{3,2,1,0:T(1,128)S(1)}, u32[]{:S(2)}, u32[]{:S(2)}) collective-permute-start(s32[2,1,1,8]{3,2,1,0:T(1,128)} %peak_ref.1), channel_id=1, source_target_pairs={{0,0},{64,64},{128,128},{192,192},{65,1},{129,65},{193,129},{1,193... | collective-permute-start | bytes 200 | tf_op jit(solution)/shard_map/ppermute | solution.py:143
  6.6 2.4 %collective-permute-done.pk_ref = s32[2,1,1,8]{3,2,1,0:T(1,128)S(1)} collective-permute-done((s32[2,1,1,8]{3,2,1,0:T(1,128)}, s32[2,1,1,8]{3,2,1,0:T(1,128)S(1)}, u32[]{:S(2)}, u32[]{:S(2)}) %collective-permute-start) | collective-permute-done | bytes 96 | tf_op jit(solution)/shard_map/ppermute | solution.py:143
  9.1 0.0 copy-start.3
  9.1 0.0 collective-permute-done.1.got_ref
  9.1 0.6 %copy-done.3 = s32[2,1,1,8]{3,2,1,0:T(1,128)} copy-done((s32[2,1,1,8]{3,2,1,0:T(1,128)}, s32[2,1,1,8]{3,2,1,0:T(1,128)S(1)}, u32[]{:S(2)}) %copy-start.3) | copy-done | bytes 88
  9.6 0.0 copy-start
  9.6 0.7 %copy-done = bf16[1,128,1024]{2,1,0:T(8,128)(2,1)} copy-done((bf16[1,128,1024]{2,1,0:T(8,128)(2,1)}, bf16[1,128,1024]{2,1,0:T(8,128)(2,1)S(1)}, u32[]{:S(2)}) %copy-start) | copy-done | bytes 262168
  10.3 2.5 %shard_map.59 = f32[32,1,128]{2,1,0:T(1,128)} custom-call(s32[2,1,1,8]{3,2,1,0:T(1,128)} %copy-done.3, bf16[1,128,1024]{2,1,0:T(8,128)(2,1)} %own_ref.1, bf16[1,128,1024]{2,1,0:T(8,128)(2,1)} %copy-done, s32[2,1,1,8]{3,2,1,0:T(1,128)} %peak_ref.1, s32[1,1,8]{2,1,0:T(1,128)} %conf_ref.1, s32[1,1,8]{2,1,0:T(1,128)} %mask_ref.1), custom_call_target="tpu_custom_call" | custom-call | tf_op jit(solution)/shard_map/pallas_call | solution.py:146
  12.8 13.2 %all_to_all.5.own_ref = f32[32,1,128]{2,1,0:T(1,128)S(1)} all-to-all(f32[32,1,128]{2,1,0:T(1,128)} %shard_map.59), channel_id=1, replica_groups={{0,1,2,3,4,5,6,7,64,65,66,67,68,69,70,71,128,129,130,131,132,133,134,13..., dimensions={0} | all-to-all | bytes 32768 | tf_op jit(solution)/shard_map/all_to_all | solution.py:157
  26.0 0.0 copy-start.1
  26.0 1.6 %collective-permute-start.2 = (f32[32,1,128]{2,1,0:T(1,128)S(1)}, f32[32,1,128]{2,1,0:T(1,128)S(1)}, u32[]{:S(2)}, u32[]{:S(2)}) collective-permute-start(f32[32,1,128]{2,1,0:T(1,128)S(1)} %all_to_all.5.own_ref), channel_id=1, source_target_pairs={{0,8},{1,9},{2,10},{3,11},{4,60},{5,61},{6,62},{7,63},{8,16},{9,17... | collective-permute-start | bytes 49160 | tf_op jit(solution)/shard_map/ppermute | solution.py:163
  27.7 5.1 %collective-permute-done.2.got_ref = f32[32,1,128]{2,1,0:T(1,128)S(1)} collective-permute-done((f32[32,1,128]{2,1,0:T(1,128)S(1)}, f32[32,1,128]{2,1,0:T(1,128)S(1)}, u32[]{:S(2)}, u32[]{:S(2)}) %collective-permute-start.2) | collective-permute-done | bytes 16416 | tf_op jit(solution)/shard_map/ppermute | solution.py:163
  32.7 0.0 copy-done.1
  32.7 0.0 copy-start.2
  32.7 0.6 %copy-done.2 = f32[32,1,128]{2,1,0:T(1,128)} copy-done((f32[32,1,128]{2,1,0:T(1,128)}, f32[32,1,128]{2,1,0:T(1,128)S(1)}, u32[]{:S(2)}) %copy-start.2) | copy-done | bytes 16408
  33.3 1.9 %shard_map.60 = (f32[2,1,1,8]{3,2,1,0:T(1,128)}, f32[2,1,1,8]{3,2,1,0:T(1,128)}) custom-call(f32[32,1,128]{2,1,0:T(1,128)} %copy-done.1, f32[32,1,128]{2,1,0:T(1,128)} %copy-done.2), custom_call_target="tpu_custom_call" | custom-call | tf_op jit(solution)/shard_map/pallas_call | solution.py:165
Async XLA Ops:
  0.6 8.5 %collective-permute-start.1 = (bf16[1,128,1024]{2,1,0:T(8,128)(2,1)}, bf16[1,128,1024]{2,1,0:T(8,128)(2,1)S(1)}, u32[]{:S(2)}, u32[]{:S(2)}) collective-permute-start(bf16[1,128,1024]{2,1,0:T(8,128)(2,1)} %own_ref.1), channel_id=1, source_target_pairs={{0,64},{64,128},{128,192},{192,0},{65,1},{129,65},{193,129},{1,193... | collective-permute-start | bytes 786440 | tf_op jit(solution)/shard_map/ppermute | solution.py:142
  4.3 4.8 %collective-permute-start = (s32[2,1,1,8]{3,2,1,0:T(1,128)}, s32[2,1,1,8]{3,2,1,0:T(1,128)S(1)}, u32[]{:S(2)}, u32[]{:S(2)}) collective-permute-start(s32[2,1,1,8]{3,2,1,0:T(1,128)} %peak_ref.1), channel_id=1, source_target_pairs={{0,0},{64,64},{128,128},{192,192},{65,1},{129,65},{193,129},{1,193... | collective-permute-start | bytes 200 | tf_op jit(solution)/shard_map/ppermute | solution.py:143
  9.1 0.6 %copy-start.3 = (s32[2,1,1,8]{3,2,1,0:T(1,128)}, s32[2,1,1,8]{3,2,1,0:T(1,128)S(1)}, u32[]{:S(2)}) copy-start(s32[2,1,1,8]{3,2,1,0:T(1,128)S(1)} %collective-permute-done.pk_ref) | copy-start | bytes 196
  9.6 0.7 %copy-start = (bf16[1,128,1024]{2,1,0:T(8,128)(2,1)}, bf16[1,128,1024]{2,1,0:T(8,128)(2,1)S(1)}, u32[]{:S(2)}) copy-start(bf16[1,128,1024]{2,1,0:T(8,128)(2,1)S(1)} %collective-permute-done.1.got_ref) | copy-start | bytes 786436
  26.0 6.7 %copy-start.1 = (f32[32,1,128]{2,1,0:T(1,128)}, f32[32,1,128]{2,1,0:T(1,128)S(1)}, u32[]{:S(2)}) copy-start(f32[32,1,128]{2,1,0:T(1,128)S(1)} %all_to_all.5.own_ref) | copy-start | bytes 49156
  26.0 6.7 %collective-permute-start.2 = (f32[32,1,128]{2,1,0:T(1,128)S(1)}, f32[32,1,128]{2,1,0:T(1,128)S(1)}, u32[]{:S(2)}, u32[]{:S(2)}) collective-permute-start(f32[32,1,128]{2,1,0:T(1,128)S(1)} %all_to_all.5.own_ref), channel_id=1, source_target_pairs={{0,8},{1,9},{2,10},{3,11},{4,60},{5,61},{6,62},{7,63},{8,16},{9,17... | collective-permute-start | bytes 49160 | tf_op jit(solution)/shard_map/ppermute | solution.py:163
  32.7 0.6 %copy-start.2 = (f32[32,1,128]{2,1,0:T(1,128)}, f32[32,1,128]{2,1,0:T(1,128)S(1)}, u32[]{:S(2)}) copy-start(f32[32,1,128]{2,1,0:T(1,128)S(1)} %collective-permute-done.2.got_ref) | copy-start | bytes 49156

commit v2 on v1

v2 whole, which is shorter than its diff:
```python
import jax
import jax.numpy as jnp
from jax import lax
from jax.experimental import pallas as pl
from jax.experimental.pallas import tpu as pltpu
from jax.sharding import PartitionSpec as P

PATCH = 128
LANES = 128
COLS = 8
ITERS = 4
STEP_SIZE = 0.12
PLANE = 8
REACH = 3
EDGE = 8
MIB = 1024 * 1024


def place():
    gz = lax.axis_index("gz")
    xy = lax.axis_index("xy")
    return gz, xy


def prepare_kernel(own_ref, conf_ref, mask_ref, shifted_ref, stiff_ref):
    for j in range(COLS):
        own = own_ref[0, :, j * PATCH : (j + 1) * PATCH].astype(jnp.float32)
        for v in range(2 * REACH + 1):
            moved = own if v == REACH else pltpu.roll(own, (REACH - v) % PATCH, 1)
            shifted_ref[v, j, EDGE : EDGE + PATCH, :] = moved
            shifted_ref[v, j, 0:EDGE, :] = moved[PATCH - EDGE :, :]
            shifted_ref[v, j, EDGE + PATCH :, :] = moved[0:EDGE, :]
    gz, _ = place()
    stiff = conf_ref[0].astype(jnp.float32) * 0.25 * mask_ref[0].astype(jnp.float32)
    stiff = stiff * (gz > 0).astype(jnp.float32)
    gap = jnp.zeros((1, 48), jnp.float32)
    stiff = jnp.concatenate([gap, gap[:, :16], stiff, stiff, gap], axis=1)
    stiff_ref[...] = pltpu.roll(stiff, gz * 16, 1)


def correlate_kernel(shifted_ref, got_ref, peak_ref, stiff_ref, out_ref):
    gz, xy = place()
    odd = lax.rem(xy, 2)
    sign = 1 - 2 * odd
    target = lax.rem(gz + odd, 4)
    peaks = [peak_ref[0, 0], peak_ref[1, 0]]
    sums = []
    for j in range(COLS):
        got = got_ref[0, :, j * PATCH : (j + 1) * PATCH].astype(jnp.float32)
        down = EDGE + sign * peaks[0][0, j]
        right = REACH + sign * peaks[1][0, j]
        sums.append(
            [
                jnp.sum(
                    jnp.sum(
                        (shifted_ref[right + v, j, pl.ds(down + u, PATCH), :] * got).reshape(
                            PATCH // 8, 8, LANES
                        ),
                        axis=0,
                    ),
                    axis=0,
                    keepdims=True,
                )
                for u, v in ((0, 0), (1, 0), (-1, 0), (0, 1), (0, -1))
            ]
        )
    scores = []
    for k in range(5):
        stacked = jnp.concatenate([sums[j][k] for j in range(COLS)], axis=0)
        scores.append(jnp.sum(stacked, axis=1, keepdims=True) * (1.0 / PATCH))
    center, y_plus, y_minus, x_plus, x_minus = scores
    scale = jnp.where(target > 0, sign, 0).astype(jnp.float32)
    delta_y = scale * (y_plus - y_minus) / (jnp.abs(y_minus) + jnp.abs(center) + jnp.abs(y_plus) + 1.0)
    delta_x = scale * (x_plus - x_minus) / (jnp.abs(x_minus) + jnp.abs(center) + jnp.abs(x_plus) + 1.0)
    lane = lax.broadcasted_iota(jnp.int32, (COLS, LANES), 1)
    patch = lax.broadcasted_iota(jnp.int32, (COLS, LANES), 0)
    spread = jnp.where(lane == patch, delta_y, 0.0)
    spread = spread + jnp.where(lane == COLS + patch, delta_x, 0.0)
    gap = jnp.zeros((1, LANES - 2 * COLS), jnp.float32)
    flow = [peaks[0].astype(jnp.float32), peaks[1].astype(jnp.float32), gap]
    flow = jnp.concatenate(flow, axis=1) + jnp.sum(spread, axis=0, keepdims=True)
    row = stiff_ref[...] + pltpu.roll(flow, target * 16, 1)
    out_ref[...] = jnp.broadcast_to(row[None], out_ref.shape)


def relax_kernel(own_ref, got_ref, flow_ref, corr_ref):
    gz, xy = place()
    z = xy // PLANE
    inner = lax.rem(xy, PLANE)
    upper = inner < PLANE // 2

    def folded(ref):
        parts = [ref[g * PLANE : (g + 1) * PLANE, 0, :] for g in range(4)]
        return (parts[0] + parts[1]) + (parts[2] + parts[3])

    own = folded(own_ref)
    got = folded(got_ref)
    window = jnp.concatenate([jnp.where(upper, got, own), jnp.where(upper, own, got)], axis=0)
    base = jnp.where(upper, z - 1, z) * PLANE
    here = jnp.where(upper, PLANE + inner, inner)
    shape = (2 * PLANE, LANES)
    lane = lax.broadcasted_iota(jnp.int32, shape, 1)
    local = lax.broadcasted_iota(jnp.int32, shape, 0)
    row = local + base
    col = lax.rem(lane, COLS)
    has_up = row > 0
    has_down = row < 63
    has_left = col > 0
    has_right = col < COLS - 1
    flow = jnp.where(lane < 64, window, 0.0)
    stiff = jnp.where(lane < 64, pltpu.roll(window, 64, 1), 0.0)
    next_stiff = jnp.where(lane < 48, pltpu.roll(stiff, LANES - 16, 1), 0.0)
    next_flow = jnp.where(lane < 48, pltpu.roll(flow, LANES - 16, 1), 0.0)
    start = flow + jnp.where(lane >= 16, pltpu.roll(flow, 16, 1), 0.0)
    start = start + jnp.where(lane >= 32, pltpu.roll(start, 32, 1), 0.0)
    nodes = start
    for _ in range(ITERS):
        force = jnp.where(has_up, pltpu.roll(nodes, 1, 0) - nodes, 0.0)
        force = force + jnp.where(has_down, pltpu.roll(nodes, 2 * PLANE - 1, 0) - nodes, 0.0)
        force = force + jnp.where(has_left, pltpu.roll(nodes, 1, 1) - nodes, 0.0)
        force = force + jnp.where(has_right, pltpu.roll(nodes, LANES - 1, 1) - nodes, 0.0)
        force = force + stiff * (pltpu.roll(nodes, 16, 1) + flow - nodes)
        force = force + next_stiff * (pltpu.roll(nodes, LANES - 16, 1) - next_flow - nodes)
        nodes = nodes + STEP_SIZE * force
    turn = lax.rem(LANES - gz * 16, LANES)
    for value, ref in ((flow, flow_ref), (nodes - start, corr_ref)):
        mine = jnp.sum(jnp.where(local == here, value, 0.0), axis=0, keepdims=True)
        mine = pltpu.roll(mine, turn, 1)
        ref[0, 0] = mine[:, 0:COLS]
        ref[1, 0] = mine[:, COLS : 2 * COLS]


def routes(groups, strips):
    half = PLANE // 2
    last = strips // PLANE - 1
    swap, fetch, hop = [], [], []
    for group in range(groups):
        for strip in range(strips):
            this = group * strips + strip
            if strip % 2 == 0:
                swap.append((this, this + strips if group < groups - 1 else this + 1))
                fetch.append((this, this))
            else:
                swap.append((this, this - strips if group > 0 else this - 1))
                fetch.append((this, (group - 1) % groups * strips + strip))
            plane, inner = divmod(strip, PLANE)
            if inner < half:
                hop.append((this, this + PLANE if plane < last else this + half))
            else:
                hop.append((this, this - PLANE if plane > 0 else this - half))
    return swap, fetch, hop


def on_device(sections, peak_offsets, confidence, tissue_mask):
    groups = lax.axis_size("gz")
    strips = lax.axis_size("xy")
    swap, fetch, hop = routes(groups, strips)
    got = lax.ppermute(sections, ("gz", "xy"), swap)
    peaks = lax.ppermute(peak_offsets, ("gz", "xy"), fetch)
    vmem = pl.BlockSpec(memory_space=pltpu.VMEM)
    shifted, stiff = pl.pallas_call(
        prepare_kernel,
        out_shape=(
            jax.ShapeDtypeStruct((2 * REACH + 1, COLS, PATCH + 2 * EDGE, LANES), jnp.float32),
            jax.ShapeDtypeStruct((1, LANES), jnp.float32),
        ),
        in_specs=[vmem, vmem, vmem],
        out_specs=(vmem, vmem),
        compiler_params=pltpu.CompilerParams(vmem_limit_bytes=8 * MIB),
    )(sections, confidence, tissue_mask)
    row = pl.pallas_call(
        correlate_kernel,
        out_shape=jax.ShapeDtypeStruct((32, 1, LANES), jnp.float32),
        in_specs=[vmem, vmem, vmem, vmem],
        out_specs=vmem,
        compiler_params=pltpu.CompilerParams(vmem_limit_bytes=8 * MIB),
    )(shifted, got, peaks, stiff)
    planes = [
        [group * strips + plane * PLANE + inner for group in range(groups) for inner in range(PLANE)]
        for plane in range(strips // PLANE)
    ]
    block = lax.all_to_all(row, ("gz", "xy"), 0, 0, axis_index_groups=planes, tiled=True)
    beside = lax.ppermute(block, ("gz", "xy"), hop)
    shape = jax.ShapeDtypeStruct(peak_offsets.shape, jnp.float32)
    return pl.pallas_call(
        relax_kernel,
        out_shape=(shape, shape),
        in_specs=[vmem, vmem],
        out_specs=(vmem, vmem),
        compiler_params=pltpu.CompilerParams(vmem_limit_bytes=4 * MIB),
    )(block, beside)


def solution(mesh):
    in_specs = (
        P("gz", "xy", None),
        P(None, "gz", "xy", None),
        P("gz", "xy", None),
        P("gz", "xy", None),
    )
    out_specs = (P(None, "gz", "xy", None), P(None, "gz", "xy", None))
    return jax.shard_map(
        on_device, mesh=mesh, in_specs=in_specs, out_specs=out_specs, check_vma=False
    )
```

time: 35.5 us -> 28.7 us (0.81)
  waiting for transfers between devices: 7.51 us -> 2.45 us
  Pallas kernels: 4.43 us -> 2.33 us
  local copies, waits for them, and re-layouts: 1.86 us -> 2.25 us
    ppermute x1, waiting for transfers between devices: 5.07 us -> 2.44 us  [on_device(): beside = lax.ppermute(block, ('gz', 'xy'), hop)]
    ppermute x1, waiting for transfers between devices: 2.44 us -> 0.01 us  [on_device(): peaks = lax.ppermute(peak_offsets, ('gz', 'xy'), fetch)]
    pallas_call x1, Pallas kernels: 2.51 us -> 0.63 us  [on_device(): pl.pallas_call(correlate_kernel, out_shape=jax.ShapeDtypeStruct((32, 1, L...]
    pallas_call x1, Pallas kernels: 1.92 us -> 1.19 us  [on_device(): pl.pallas_call(relax_kernel, out_shape=(shape, shape), in_specs=[vmem, vm...]
    pallas_call x0 -> x1, Pallas kernels: none -> 0.51 us  [on_device(): pl.pallas_call(prepare_kernel, out_shape=(jax.ShapeDtypeStruct((2 * REACH...]
    unnamed x8 -> x6, local copies, waits for them, and re-layouts: 1.86 us -> 2.25 us
    ppermute x1, starting transfers between devices: 3.64 us -> 3.26 us  [on_device(): got = lax.ppermute(sections, ('gz', 'xy'), swap)]
  transfers between devices with their start and end apart: 3 -> 3, of which waited for: 2 -> 1; matrix products, arithmetic and copies ran while one was open for 0% -> 0% of each run, Pallas kernels for 0% -> 2%
where the time goes in v2:
time: 28.7 us; the launch traced here: 28.5 us
  blocking collectives  13.2 us (46%)
  starting transfers between devices  7.59 us (26%)
  waiting for transfers between devices  2.45 us (9%)
  Pallas kernels  2.33 us (8%)
  local copies, waits for them, and re-layouts  2.25 us (8%)
  between operations  0.66 us (2%)
    all_to_all x1, blocking collectives, on_device(): lax.all_to_all(row, ('gz', 'xy'), 0, 0, axis_index_groups=planes, tiled=T...  13.2 us
    ppermute x1, starting transfers between devices, on_device(): got = lax.ppermute(sections, ('gz', 'xy'), swap)  3.26 us
    ppermute x1, starting transfers between devices, on_device(): peaks = lax.ppermute(peak_offsets, ('gz', 'xy'), fetch)  2.68 us
    ppermute x1, waiting for transfers between devices, on_device(): beside = lax.ppermute(block, ('gz', 'xy'), hop)  2.44 us
    unnamed x6, local copies, waits for them, and re-layouts  2.25 us
    ppermute x1, starting transfers between devices, on_device(): beside = lax.ppermute(block, ('gz', 'xy'), hop)  1.65 us
    pallas_call x1, Pallas kernels, on_device(): pl.pallas_call(relax_kernel, out_shape=(shape, shape), in_specs=[vmem, vm...  1.19 us
    pallas_call x1, Pallas kernels, on_device(): pl.pallas_call(correlate_kernel, out_shape=jax.ShapeDtypeStruct((32, 1, L...  0.63 us
  transfers between devices with their start and end apart: 3, of which 1 were waited for; matrix products, arithmetic and copies ran while one was open for 0% of the time, Pallas kernels for 2%

profile of v2, /device:TPU:1, one launch (start us, length us, event | category | flops | bytes accessed | tf_op | source)
XLA Modules:
  0.0 28.5 jit_solution(10207795827866181630)
XLA Ops:
  0.6 3.3 %collective-permute-start = (bf16[1,128,1024]{2,1,0:T(8,128)(2,1)}, bf16[1,128,1024]{2,1,0:T(8,128)(2,1)S(1)}, u32[]{:S(2)}, u32[]{:S(2)}) collective-permute-start(bf16[1,128,1024]{2,1,0:T(8,128)(2,1)} %own_ref.1), channel_id=1, source_target_pairs={{0,64},{1,0},{2,66},{3,2},{4,68},{5,4},{6,70},{7,6},{8,72},{9,8},{... | collective-permute-start | bytes 786440 | tf_op jit(solution)/shard_map/ppermute | solution.py:158
  3.9 2.7 %collective-permute-start.1 = (s32[2,1,1,8]{3,2,1,0:T(1,128)}, s32[2,1,1,8]{3,2,1,0:T(1,128)S(1)}, u32[]{:S(2)}, u32[]{:S(2)}) collective-permute-start(s32[2,1,1,8]{3,2,1,0:T(1,128)} %param.5), channel_id=1, source_target_pairs={{0,0},{1,193},{2,2},{3,195},{4,4},{5,197},{6,6},{7,199},{8,8},{9,2... | collective-permute-start | bytes 200 | tf_op jit(solution)/shard_map/ppermute | solution.py:159
  6.6 0.0 copy-start
  6.6 0.9 %copy-done = bf16[1,128,1024]{2,1,0:T(8,128)(2,1)S(1)} copy-done((bf16[1,128,1024]{2,1,0:T(8,128)(2,1)S(1)}, bf16[1,128,1024]{2,1,0:T(8,128)(2,1)}, u32[]{:S(2)}) %copy-start) | copy-done | bytes 262168
  7.5 0.0 copy-start.1
  7.5 0.7 %copy-done.1 = s32[1,1,8]{2,1,0:T(1,128)S(1)} copy-done((s32[1,1,8]{2,1,0:T(1,128)S(1)}, s32[1,1,8]{2,1,0:T(1,128)}, u32[]{:S(2)}) %copy-start.1) | copy-done | bytes 56
  8.2 0.0 copy-start.2
  8.2 0.7 %copy-done.2 = s32[1,1,8]{2,1,0:T(1,128)S(1)} copy-done((s32[1,1,8]{2,1,0:T(1,128)S(1)}, s32[1,1,8]{2,1,0:T(1,128)}, u32[]{:S(2)}) %copy-start.2) | copy-done | bytes 56
  8.8 0.5 %shard_map.59 = (f32[7,8,144,128]{3,2,1,0:T(8,128)S(1)}, f32[1,128]{1,0:T(1,128)S(1)}) custom-call(bf16[1,128,1024]{2,1,0:T(8,128)(2,1)S(1)} %copy-done, s32[1,1,8]{2,1,0:T(1,128)S(1)} %copy-done.1, s32[1,1,8]{2,1,0:T(1,128)S(1)} %copy-done.2), custom_call_target="tpu_custom_call" | custom-call | tf_op jit(solution)/shard_map/pallas_call | solution.py:161
  9.3 0.0 collective-permute-done.1.peak_ref
  9.4 0.0 collective-permute-done.got_ref
  9.4 0.6 %shard_map.60 = f32[32,1,128]{2,1,0:T(1,128)S(1)} custom-call(f32[7,8,144,128]{3,2,1,0:T(8,128)S(1)} %get-tuple-element.4.shifted_ref, bf16[1,128,1024]{2,1,0:T(8,128)(2,1)S(1)} %collective-permute-done.got_ref, s32[2,1,1,8]{3,2,1,0:T(1,128)S(1)} %collective-permute-done.1.peak_ref, f32[1,128]{1,0:T(1,128)S(1)} %get-tuple-element.5.stiff_ref), custom_call_target="tpu_custom_call" | custom-call | tf_op jit(solution)/shard_map/pallas_call | solution.py:171
  10.0 13.2 %all_to_all.5.own_ref = f32[32,1,128]{2,1,0:T(1,128)S(1)} all-to-all(f32[32,1,128]{2,1,0:T(1,128)S(1)} %shard_map.60), channel_id=1, replica_groups={{0,1,2,3,4,5,6,7,64,65,66,67,68,69,70,71,128,129,130,131,132,133,134,13..., dimensions={0} | all-to-all | bytes 32768 | tf_op jit(solution)/shard_map/all_to_all | solution.py:182
  23.2 1.6 %collective-permute-start.2 = (f32[32,1,128]{2,1,0:T(1,128)S(1)}, f32[32,1,128]{2,1,0:T(1,128)S(1)}, u32[]{:S(2)}, u32[]{:S(2)}) collective-permute-start(f32[32,1,128]{2,1,0:T(1,128)S(1)} %all_to_all.5.own_ref), channel_id=1, source_target_pairs={{0,8},{1,9},{2,10},{3,11},{4,0},{5,1},{6,2},{7,3},{8,16},{9,17},{1... | collective-permute-start | bytes 49160 | tf_op jit(solution)/shard_map/ppermute | solution.py:183
  24.8 2.4 %collective-permute-done.2.got_ref = f32[32,1,128]{2,1,0:T(1,128)S(1)} collective-permute-done((f32[32,1,128]{2,1,0:T(1,128)S(1)}, f32[32,1,128]{2,1,0:T(1,128)S(1)}, u32[]{:S(2)}, u32[]{:S(2)}) %collective-permute-start.2) | collective-permute-done | bytes 16416 | tf_op jit(solution)/shard_map/ppermute | solution.py:183
  27.3 1.2 %shard_map.61 = (f32[2,1,1,8]{3,2,1,0:T(1,128)}, f32[2,1,1,8]{3,2,1,0:T(1,128)}) custom-call(f32[32,1,128]{2,1,0:T(1,128)S(1)} %all_to_all.5.own_ref, f32[32,1,128]{2,1,0:T(1,128)S(1)} %collective-permute-done.2.got_ref), custom_call_target="tpu_custom_call" | custom-call | tf_op jit(solution)/shard_map/pallas_call | solution.py:185
Async XLA Ops:
  0.6 8.7 %collective-permute-start = (bf16[1,128,1024]{2,1,0:T(8,128)(2,1)}, bf16[1,128,1024]{2,1,0:T(8,128)(2,1)S(1)}, u32[]{:S(2)}, u32[]{:S(2)}) collective-permute-start(bf16[1,128,1024]{2,1,0:T(8,128)(2,1)} %own_ref.1), channel_id=1, source_target_pairs={{0,64},{1,0},{2,66},{3,2},{4,68},{5,4},{6,70},{7,6},{8,72},{9,8},{... | collective-permute-start | bytes 786440 | tf_op jit(solution)/shard_map/ppermute | solution.py:158
  3.9 5.5 %collective-permute-start.1 = (s32[2,1,1,8]{3,2,1,0:T(1,128)}, s32[2,1,1,8]{3,2,1,0:T(1,128)S(1)}, u32[]{:S(2)}, u32[]{:S(2)}) collective-permute-start(s32[2,1,1,8]{3,2,1,0:T(1,128)} %param.5), channel_id=1, source_target_pairs={{0,0},{1,193},{2,2},{3,195},{4,4},{5,197},{6,6},{7,199},{8,8},{9,2... | collective-permute-start | bytes 200 | tf_op jit(solution)/shard_map/ppermute | solution.py:159
  6.6 1.0 %copy-start = (bf16[1,128,1024]{2,1,0:T(8,128)(2,1)S(1)}, bf16[1,128,1024]{2,1,0:T(8,128)(2,1)}, u32[]{:S(2)}) copy-start(bf16[1,128,1024]{2,1,0:T(8,128)(2,1)} %own_ref.1) | copy-start | bytes 786436
  7.5 0.7 %copy-start.1 = (s32[1,1,8]{2,1,0:T(1,128)S(1)}, s32[1,1,8]{2,1,0:T(1,128)}, u32[]{:S(2)}) copy-start(s32[1,1,8]{2,1,0:T(1,128)} %conf_ref.1) | copy-start | bytes 100
  8.2 0.7 %copy-start.2 = (s32[1,1,8]{2,1,0:T(1,128)S(1)}, s32[1,1,8]{2,1,0:T(1,128)}, u32[]{:S(2)}) copy-start(s32[1,1,8]{2,1,0:T(1,128)} %mask_ref.1) | copy-start | bytes 100
  23.2 4.1 %collective-permute-start.2 = (f32[32,1,128]{2,1,0:T(1,128)S(1)}, f32[32,1,128]{2,1,0:T(1,128)S(1)}, u32[]{:S(2)}, u32[]{:S(2)}) collective-permute-start(f32[32,1,128]{2,1,0:T(1,128)S(1)} %all_to_all.5.own_ref), channel_id=1, source_target_pairs={{0,8},{1,9},{2,10},{3,11},{4,0},{5,1},{6,2},{7,3},{8,16},{9,17},{1... | collective-permute-start | bytes 49160 | tf_op jit(solution)/shard_map/ppermute | solution.py:183

commit v3 on v2

--- a/solution.py
+++ b/solution.py
@@ -22,7 +22,8 @@
     return gz, xy
 
 
-def prepare_kernel(own_ref, conf_ref, mask_ref, shifted_ref, stiff_ref):
+def prepare_kernel(own_ref, peak_ref, conf_ref, mask_ref, shifted_ref, stiff_ref, kept_ref):
+    kept_ref[...] = peak_ref[...]
     for j in range(COLS):
         own = own_ref[0, :, j * PATCH : (j + 1) * PATCH].astype(jnp.float32)
         for v in range(2 * REACH + 1):
@@ -38,12 +39,12 @@
     stiff_ref[...] = pltpu.roll(stiff, gz * 16, 1)
 
 
-def correlate_kernel(shifted_ref, got_ref, peak_ref, stiff_ref, out_ref):
+def correlate_kernel(shifted_ref, got_ref, kept_ref, sent_ref, stiff_ref, out_ref):
     gz, xy = place()
     odd = lax.rem(xy, 2)
     sign = 1 - 2 * odd
     target = lax.rem(gz + odd, 4)
-    peaks = [peak_ref[0, 0], peak_ref[1, 0]]
+    peaks = [jnp.where(odd > 0, sent_ref[i, 0], kept_ref[i, 0]) for i in range(2)]
     sums = []
     for j in range(COLS):
         got = got_ref[0, :, j * PATCH : (j + 1) * PATCH].astype(jnp.float32)
@@ -89,12 +90,8 @@
     inner = lax.rem(xy, PLANE)
     upper = inner < PLANE // 2
 
-    def folded(ref):
-        parts = [ref[g * PLANE : (g + 1) * PLANE, 0, :] for g in range(4)]
-        return (parts[0] + parts[1]) + (parts[2] + parts[3])
-
-    own = folded(own_ref)
-    got = folded(got_ref)
+    own = own_ref[...]
+    got = got_ref[...]
     window = jnp.concatenate([jnp.where(upper, got, own), jnp.where(upper, own, got)], axis=0)
     base = jnp.where(upper, z - 1, z) * PLANE
     here = jnp.where(upper, PLANE + inner, inner)
@@ -131,7 +128,6 @@
 
 
 def routes(groups, strips):
-    half = PLANE // 2
     last = strips // PLANE - 1
     swap, fetch, hop = [], [], []
     for group in range(groups):
@@ -139,15 +135,17 @@
             this = group * strips + strip
             if strip % 2 == 0:
                 swap.append((this, this + strips if group < groups - 1 else this + 1))
-                fetch.append((this, this))
+                fetch.append((this, group * strips + (strip ^ 2)))
             else:
                 swap.append((this, this - strips if group > 0 else this - 1))
                 fetch.append((this, (group - 1) % groups * strips + strip))
             plane, inner = divmod(strip, PLANE)
-            if inner < half:
-                hop.append((this, this + PLANE if plane < last else this + half))
+            twin = this ^ 1
+            turn = this - inner + PLANE - 2 - inner // 2 * 2 + inner % 2
+            if inner < PLANE // 2:
+                hop.append((this, twin + PLANE if plane < last else turn))
             else:
-                hop.append((this, this - PLANE if plane > 0 else this - half))
+                hop.append((this, twin - PLANE if plane > 0 else turn))
     return swap, fetch, hop
 
 
@@ -156,30 +154,32 @@
     strips = lax.axis_size("xy")
     swap, fetch, hop = routes(groups, strips)
     got = lax.ppermute(sections, ("gz", "xy"), swap)
-    peaks = lax.ppermute(peak_offsets, ("gz", "xy"), fetch)
+    sent = lax.ppermute(peak_offsets, ("gz", "xy"), fetch)
     vmem = pl.BlockSpec(memory_space=pltpu.VMEM)
-    shifted, stiff = pl.pallas_call(
+    shifted, stiff, kept = pl.pallas_call(
         prepare_kernel,
         out_shape=(
             jax.ShapeDtypeStruct((2 * REACH + 1, COLS, PATCH + 2 * EDGE, LANES), jnp.float32),
             jax.ShapeDtypeStruct((1, LANES), jnp.float32),
+            jax.ShapeDtypeStruct(peak_offsets.shape, jnp.int32),
         ),
-        in_specs=[vmem, vmem, vmem],
-        out_specs=(vmem, vmem),
+        in_specs=[vmem, vmem, vmem, vmem],
+        out_specs=(vmem, vmem, vmem),
         compiler_params=pltpu.CompilerParams(vmem_limit_bytes=8 * MIB),
-    )(sections, confidence, tissue_mask)
+    )(sections, peak_offsets, confidence, tissue_mask)
     row = pl.pallas_call(
         correlate_kernel,
         out_shape=jax.ShapeDtypeStruct((32, 1, LANES), jnp.float32),
-        in_specs=[vmem, vmem, vmem, vmem],
+        in_specs=[vmem, vmem, vmem, vmem, vmem],
         out_specs=vmem,
         compiler_params=pltpu.CompilerParams(vmem_limit_bytes=8 * MIB),
-    )(shifted, got, peaks, stiff)
+    )(shifted, got, kept, sent, stiff)
     planes = [
         [group * strips + plane * PLANE + inner for group in range(groups) for inner in range(PLANE)]
         for plane in range(strips // PLANE)
     ]
     block = lax.all_to_all(row, ("gz", "xy"), 0, 0, axis_index_groups=planes, tiled=True)
+    block = jnp.sum(block.reshape(groups, PLANE, LANES), axis=0)
     beside = lax.ppermute(block, ("gz", "xy"), hop)
     shape = jax.ShapeDtypeStruct(peak_offsets.shape, jnp.float32)
     return pl.pallas_call(

time: 28.7 us -> 28.2 us (0.983)
  starting transfers between devices: 7.59 us -> 6.22 us
  blocking collectives: 13.2 us -> 14.4 us
  waiting for transfers between devices: 2.45 us -> 1.49 us
  local copies, waits for them, and re-layouts: 2.25 us -> 2.94 us
    ppermute x1, starting transfers between devices: 2.68 us -> 0.79 us  [on_device(): sent = lax.ppermute(peak_offsets, ('gz', 'xy'), fetch)]
    all_to_all x1, blocking collectives: 13.2 us -> 14.4 us  [on_device(): lax.all_to_all(row, ('gz', 'xy'), 0, 0, axis_index_groups=planes, tiled=T...]
    ppermute x1, waiting for transfers between devices: 2.44 us -> 1.49 us  [on_device(): beside = lax.ppermute(block, ('gz', 'xy'), hop)]
    unnamed x6 -> x8, local copies, waits for them, and re-layouts: 2.25 us -> 2.94 us
    ppermute x1, starting transfers between devices: 1.65 us -> 2.18 us  [on_device(): beside = lax.ppermute(block, ('gz', 'xy'), hop)]
where the time goes in v3:
time: 28.2 us; the launch traced here: 28 us
  blocking collectives  14.4 us (51%)
  starting transfers between devices  6.22 us (22%)
  local copies, waits for them, and re-layouts  2.94 us (10%)
  Pallas kernels  2.29 us (8%)
  waiting for transfers between devices  1.49 us (5%)
  between operations  0.65 us (2%)
    all_to_all x1, blocking collectives, on_device(): lax.all_to_all(row, ('gz', 'xy'), 0, 0, axis_index_groups=planes, tiled=T...  14.4 us
    ppermute x1, starting transfers between devices, on_device(): got = lax.ppermute(sections, ('gz', 'xy'), swap)  3.26 us
    unnamed x8, local copies, waits for them, and re-layouts  2.94 us
    ppermute x1, starting transfers between devices, on_device(): beside = lax.ppermute(block, ('gz', 'xy'), hop)  2.18 us
    ppermute x1, waiting for transfers between devices, on_device(): beside = lax.ppermute(block, ('gz', 'xy'), hop)  1.49 us
    pallas_call x1, Pallas kernels, on_device(): pl.pallas_call(relax_kernel, out_shape=(shape, shape), in_specs=[vmem, vm...  1.17 us
    ppermute x1, starting transfers between devices, on_device(): sent = lax.ppermute(peak_offsets, ('gz', 'xy'), fetch)  0.79 us
    pallas_call x1, Pallas kernels, on_device(): pl.pallas_call(correlate_kernel, out_shape=jax.ShapeDtypeStruct((32, 1, L...  0.6 us
  transfers between devices with their start and end apart: 3, of which 1 were waited for; matrix products, arithmetic and copies ran while one was open for 0% of the time, Pallas kernels for 2%

profile of v3, /device:TPU:1, one launch (start us, length us, event | category | flops | bytes accessed | tf_op | source)
XLA Modules:
  0.0 28.0 jit_solution(3262976419638040243)
XLA Ops:
  0.6 3.3 %collective-permute-start = (bf16[1,128,1024]{2,1,0:T(8,128)(2,1)}, bf16[1,128,1024]{2,1,0:T(8,128)(2,1)S(1)}, u32[]{:S(2)}, u32[]{:S(2)}) collective-permute-start(bf16[1,128,1024]{2,1,0:T(8,128)(2,1)} %own_ref.1), channel_id=1, source_target_pairs={{0,64},{1,0},{2,66},{3,2},{4,68},{5,4},{6,70},{7,6},{8,72},{9,8},{... | collective-permute-start | bytes 786440 | tf_op jit(solution)/shard_map/ppermute | solution.py:156
  3.9 0.8 %collective-permute-start.1 = (s32[2,1,1,8]{3,2,1,0:T(1,128)}, s32[2,1,1,8]{3,2,1,0:T(1,128)S(1)}, u32[]{:S(2)}, u32[]{:S(2)}) collective-permute-start(s32[2,1,1,8]{3,2,1,0:T(1,128)} %peak_ref.1), channel_id=1, source_target_pairs={{0,2},{1,193},{2,0},{3,195},{4,6},{5,197},{6,4},{7,199},{8,10},{9,... | collective-permute-start | bytes 200 | tf_op jit(solution)/shard_map/ppermute | solution.py:157
  4.7 0.0 copy-start
  4.7 0.9 %copy-done = bf16[1,128,1024]{2,1,0:T(8,128)(2,1)S(1)} copy-done((bf16[1,128,1024]{2,1,0:T(8,128)(2,1)S(1)}, bf16[1,128,1024]{2,1,0:T(8,128)(2,1)}, u32[]{:S(2)}) %copy-start) | copy-done | bytes 262168
  5.6 0.0 copy-start.1
  5.6 0.7 %copy-done.1 = s32[2,1,1,8]{3,2,1,0:T(1,128)S(1)} copy-done((s32[2,1,1,8]{3,2,1,0:T(1,128)S(1)}, s32[2,1,1,8]{3,2,1,0:T(1,128)}, u32[]{:S(2)}) %copy-start.1) | copy-done | bytes 88
  6.3 0.0 copy-start.2
  6.3 0.7 %copy-done.2 = s32[1,1,8]{2,1,0:T(1,128)S(1)} copy-done((s32[1,1,8]{2,1,0:T(1,128)S(1)}, s32[1,1,8]{2,1,0:T(1,128)}, u32[]{:S(2)}) %copy-start.2) | copy-done | bytes 56
  7.0 0.0 copy-start.3
  7.0 0.7 %copy-done.3 = s32[1,1,8]{2,1,0:T(1,128)S(1)} copy-done((s32[1,1,8]{2,1,0:T(1,128)S(1)}, s32[1,1,8]{2,1,0:T(1,128)}, u32[]{:S(2)}) %copy-start.3) | copy-done | bytes 56
  7.6 0.5 %shard_map.59 = (f32[7,8,144,128]{3,2,1,0:T(8,128)S(1)}, f32[1,128]{1,0:T(1,128)S(1)}, s32[2,1,1,8]{3,2,1,0:T(1,128)S(1)}) custom-call(bf16[1,128,1024]{2,1,0:T(8,128)(2,1)S(1)} %copy-done, s32[2,1,1,8]{3,2,1,0:T(1,128)S(1)} %copy-done.1, s32[1,1,8]{2,1,0:T(1,128)S(1)} %copy-done.2, s32[1,1,8]{2,1,0:T(1,128)S(1)} %copy-done.3), custom_call_target="tpu_custom_call" | custom-call | tf_op jit(solution)/shard_map/pallas_call | solution.py:159
  8.1 0.0 collective-permute-done.1.sent_ref
  8.1 0.0 collective-permute-done.got_ref
  8.1 0.6 %shard_map.60 = f32[32,1,128]{2,1,0:T(1,128)S(1)} custom-call(f32[7,8,144,128]{3,2,1,0:T(8,128)S(1)} %get-tuple-element.5.shifted_ref, bf16[1,128,1024]{2,1,0:T(8,128)(2,1)S(1)} %collective-permute-done.got_ref, s32[2,1,1,8]{3,2,1,0:T(1,128)S(1)} %get-tuple-element.6.kept_ref, s32[2,1,1,8]{3,2,1,0:T(1,128)S(1)} %collective-permute-done.1.sent_ref, ...), custom_call_target="tpu_custom_call" | custom-call | tf_op jit(solution)/shard_map/pallas_call | solution.py:170
  8.7 14.4 %all_to_all.5 = f32[32,1,128]{2,1,0:T(1,128)S(1)} all-to-all(f32[32,1,128]{2,1,0:T(1,128)S(1)} %shard_map.60), channel_id=1, replica_groups={{0,1,2,3,4,5,6,7,64,65,66,67,68,69,70,71,128,129,130,131,132,133,134,13..., dimensions={0} | all-to-all | bytes 32768 | tf_op jit(solution)/shard_map/all_to_all | solution.py:181
  23.2 2.2 %collective-permute-start.2 = (f32[8,128]{1,0:T(8,128)S(1)}, f32[8,128]{1,0:T(8,128)S(1)}, u32[]{:S(2)}, u32[]{:S(2)}) collective-permute-start(f32[8,128]{1,0:T(8,128)S(1)} %bitcast_reduce_fusion.own_ref), channel_id=1, source_target_pairs={{0,9},{1,8},{2,11},{3,10},{4,2},{5,3},{6,0},{7,1},{8,17},{9,16},{1... | collective-permute-start | bytes 12296 | tf_op jit(solution)/shard_map/ppermute | solution.py:183
  25.3 1.5 %collective-permute-done.2.got_ref = f32[8,128]{1,0:T(8,128)S(1)} collective-permute-done((f32[8,128]{1,0:T(8,128)S(1)}, f32[8,128]{1,0:T(8,128)S(1)}, u32[]{:S(2)}, u32[]{:S(2)}) %collective-permute-start.2) | collective-permute-done | bytes 4128 | tf_op jit(solution)/shard_map/ppermute | solution.py:183
  26.8 1.2 %shard_map.61 = (f32[2,1,1,8]{3,2,1,0:T(1,128)}, f32[2,1,1,8]{3,2,1,0:T(1,128)}) custom-call(f32[8,128]{1,0:T(8,128)S(1)} %bitcast_reduce_fusion.own_ref, f32[8,128]{1,0:T(8,128)S(1)} %collective-permute-done.2.got_ref), custom_call_target="tpu_custom_call" | custom-call | tf_op jit(solution)/shard_map/pallas_call | solution.py:185
  (1 shorter events, 0.0 us)
Async XLA Ops:
  0.6 7.5 %collective-permute-start = (bf16[1,128,1024]{2,1,0:T(8,128)(2,1)}, bf16[1,128,1024]{2,1,0:T(8,128)(2,1)S(1)}, u32[]{:S(2)}, u32[]{:S(2)}) collective-permute-start(bf16[1,128,1024]{2,1,0:T(8,128)(2,1)} %own_ref.1), channel_id=1, source_target_pairs={{0,64},{1,0},{2,66},{3,2},{4,68},{5,4},{6,70},{7,6},{8,72},{9,8},{... | collective-permute-start | bytes 786440 | tf_op jit(solution)/shard_map/ppermute | solution.py:156
  3.9 4.2 %collective-permute-start.1 = (s32[2,1,1,8]{3,2,1,0:T(1,128)}, s32[2,1,1,8]{3,2,1,0:T(1,128)S(1)}, u32[]{:S(2)}, u32[]{:S(2)}) collective-permute-start(s32[2,1,1,8]{3,2,1,0:T(1,128)} %peak_ref.1), channel_id=1, source_target_pairs={{0,2},{1,193},{2,0},{3,195},{4,6},{5,197},{6,4},{7,199},{8,10},{9,... | collective-permute-start | bytes 200 | tf_op jit(solution)/shard_map/ppermute | solution.py:157
  4.7 0.9 %copy-start = (bf16[1,128,1024]{2,1,0:T(8,128)(2,1)S(1)}, bf16[1,128,1024]{2,1,0:T(8,128)(2,1)}, u32[]{:S(2)}) copy-start(bf16[1,128,1024]{2,1,0:T(8,128)(2,1)} %own_ref.1) | copy-start | bytes 786436
  5.6 0.7 %copy-start.1 = (s32[2,1,1,8]{3,2,1,0:T(1,128)S(1)}, s32[2,1,1,8]{3,2,1,0:T(1,128)}, u32[]{:S(2)}) copy-start(s32[2,1,1,8]{3,2,1,0:T(1,128)} %peak_ref.1) | copy-start | bytes 196
  6.3 0.7 %copy-start.2 = (s32[1,1,8]{2,1,0:T(1,128)S(1)}, s32[1,1,8]{2,1,0:T(1,128)}, u32[]{:S(2)}) copy-start(s32[1,1,8]{2,1,0:T(1,128)} %conf_ref.1) | copy-start | bytes 100
  7.0 0.7 %copy-start.3 = (s32[1,1,8]{2,1,0:T(1,128)S(1)}, s32[1,1,8]{2,1,0:T(1,128)}, u32[]{:S(2)}) copy-start(s32[1,1,8]{2,1,0:T(1,128)} %mask_ref.1) | copy-start | bytes 100
  23.2 3.7 %collective-permute-start.2 = (f32[8,128]{1,0:T(8,128)S(1)}, f32[8,128]{1,0:T(8,128)S(1)}, u32[]{:S(2)}, u32[]{:S(2)}) collective-permute-start(f32[8,128]{1,0:T(8,128)S(1)} %bitcast_reduce_fusion.own_ref), channel_id=1, source_target_pairs={{0,9},{1,8},{2,11},{3,10},{4,2},{5,3},{6,0},{7,1},{8,17},{9,16},{1... | collective-permute-start | bytes 12296 | tf_op jit(solution)/shard_map/ppermute | solution.py:183

commit v4 on v3

--- a/solution.py
+++ b/solution.py
@@ -39,30 +39,39 @@
     stiff_ref[...] = pltpu.roll(stiff, gz * 16, 1)
 
 
-def correlate_kernel(shifted_ref, got_ref, kept_ref, sent_ref, stiff_ref, out_ref):
+def window_kernel(shifted_ref, kept_ref, sent_ref, stiff_ref, windows_ref, fixed_ref):
     gz, xy = place()
     odd = lax.rem(xy, 2)
     sign = 1 - 2 * odd
     target = lax.rem(gz + odd, 4)
     peaks = [jnp.where(odd > 0, sent_ref[i, 0], kept_ref[i, 0]) for i in range(2)]
+    for j in range(COLS):
+        down = EDGE + sign * peaks[0][0, j]
+        right = REACH + sign * peaks[1][0, j]
+        for k, (u, v) in enumerate(((0, 0), (1, 0), (-1, 0), (0, 1), (0, -1))):
+            windows_ref[k, j] = shifted_ref[right + v, j, pl.ds(down + u, PATCH), :]
+    gap = jnp.zeros((1, LANES - 2 * COLS), jnp.float32)
+    flow = [peaks[0].astype(jnp.float32), peaks[1].astype(jnp.float32), gap]
+    flow = jnp.concatenate(flow, axis=1)
+    fixed_ref[...] = stiff_ref[...] + pltpu.roll(flow, target * 16, 1)
+
+
+def correlate_kernel(windows_ref, got_ref, fixed_ref, out_ref):
+    gz, xy = place()
+    odd = lax.rem(xy, 2)
+    sign = 1 - 2 * odd
+    target = lax.rem(gz + odd, 4)
     sums = []
     for j in range(COLS):
         got = got_ref[0, :, j * PATCH : (j + 1) * PATCH].astype(jnp.float32)
-        down = EDGE + sign * peaks[0][0, j]
-        right = REACH + sign * peaks[1][0, j]
         sums.append(
             [
                 jnp.sum(
-                    jnp.sum(
-                        (shifted_ref[right + v, j, pl.ds(down + u, PATCH), :] * got).reshape(
-                            PATCH // 8, 8, LANES
-                        ),
-                        axis=0,
-                    ),
+                    jnp.sum((windows_ref[k, j] * got).reshape(PATCH // 8, 8, LANES), axis=0),
                     axis=0,
                     keepdims=True,
                 )
-                for u, v in ((0, 0), (1, 0), (-1, 0), (0, 1), (0, -1))
+                for k in range(5)
             ]
         )
     scores = []
@@ -75,12 +84,9 @@
     delta_x = scale * (x_plus - x_minus) / (jnp.abs(x_minus) + jnp.abs(center) + jnp.abs(x_plus) + 1.0)
     lane = lax.broadcasted_iota(jnp.int32, (COLS, LANES), 1)
     patch = lax.broadcasted_iota(jnp.int32, (COLS, LANES), 0)
-    spread = jnp.where(lane == patch, delta_y, 0.0)
-    spread = spread + jnp.where(lane == COLS + patch, delta_x, 0.0)
-    gap = jnp.zeros((1, LANES - 2 * COLS), jnp.float32)
-    flow = [peaks[0].astype(jnp.float32), peaks[1].astype(jnp.float32), gap]
-    flow = jnp.concatenate(flow, axis=1) + jnp.sum(spread, axis=0, keepdims=True)
-    row = stiff_ref[...] + pltpu.roll(flow, target * 16, 1)
+    spread = jnp.where(lane == target * 16 + patch, delta_y, 0.0)
+    spread = spread + jnp.where(lane == target * 16 + COLS + patch, delta_x, 0.0)
+    row = fixed_ref[...] + jnp.sum(spread, axis=0, keepdims=True)
     out_ref[...] = jnp.broadcast_to(row[None], out_ref.shape)
 
 
@@ -106,19 +112,22 @@
     has_right = col < COLS - 1
     flow = jnp.where(lane < 64, window, 0.0)
     stiff = jnp.where(lane < 64, pltpu.roll(window, 64, 1), 0.0)
-    next_stiff = jnp.where(lane < 48, pltpu.roll(stiff, LANES - 16, 1), 0.0)
-    next_flow = jnp.where(lane < 48, pltpu.roll(flow, LANES - 16, 1), 0.0)
+    next_stiff = jnp.where(lane < 48, pltpu.roll(window, 48, 1), 0.0)
+    next_flow = jnp.where(lane < 48, pltpu.roll(window, LANES - 16, 1), 0.0)
     start = flow + jnp.where(lane >= 16, pltpu.roll(flow, 16, 1), 0.0)
-    start = start + jnp.where(lane >= 32, pltpu.roll(start, 32, 1), 0.0)
+    start = start + (
+        jnp.where(lane >= 32, pltpu.roll(flow, 32, 1), 0.0)
+        + jnp.where(lane >= 48, pltpu.roll(flow, 48, 1), 0.0)
+    )
     nodes = start
     for _ in range(ITERS):
-        force = jnp.where(has_up, pltpu.roll(nodes, 1, 0) - nodes, 0.0)
-        force = force + jnp.where(has_down, pltpu.roll(nodes, 2 * PLANE - 1, 0) - nodes, 0.0)
-        force = force + jnp.where(has_left, pltpu.roll(nodes, 1, 1) - nodes, 0.0)
-        force = force + jnp.where(has_right, pltpu.roll(nodes, LANES - 1, 1) - nodes, 0.0)
-        force = force + stiff * (pltpu.roll(nodes, 16, 1) + flow - nodes)
-        force = force + next_stiff * (pltpu.roll(nodes, LANES - 16, 1) - next_flow - nodes)
-        nodes = nodes + STEP_SIZE * force
+        rows = jnp.where(has_up, pltpu.roll(nodes, 1, 0) - nodes, 0.0)
+        rows = rows + jnp.where(has_down, pltpu.roll(nodes, 2 * PLANE - 1, 0) - nodes, 0.0)
+        cols = jnp.where(has_left, pltpu.roll(nodes, 1, 1) - nodes, 0.0)
+        cols = cols + jnp.where(has_right, pltpu.roll(nodes, LANES - 1, 1) - nodes, 0.0)
+        links = stiff * (pltpu.roll(nodes, 16, 1) + flow - nodes)
+        links = links + next_stiff * (pltpu.roll(nodes, LANES - 16, 1) - next_flow - nodes)
+        nodes = nodes + STEP_SIZE * ((rows + cols) + links)
     turn = lax.rem(LANES - gz * 16, LANES)
     for value, ref in ((flow, flow_ref), (nodes - start, corr_ref)):
         mine = jnp.sum(jnp.where(local == here, value, 0.0), axis=0, keepdims=True)
@@ -167,13 +176,23 @@
         out_specs=(vmem, vmem, vmem),
         compiler_params=pltpu.CompilerParams(vmem_limit_bytes=8 * MIB),
     )(sections, peak_offsets, confidence, tissue_mask)
+    windows, fixed = pl.pallas_call(
+        window_kernel,
+        out_shape=(
+            jax.ShapeDtypeStruct((5, COLS, PATCH, LANES), jnp.float32),
+            jax.ShapeDtypeStruct((1, LANES), jnp.float32),
+        ),
+        in_specs=[vmem, vmem, vmem, vmem],
+        out_specs=(vmem, vmem),
+        compiler_params=pltpu.CompilerParams(vmem_limit_bytes=8 * MIB),
+    )(shifted, kept, sent, stiff)
     row = pl.pallas_call(
         correlate_kernel,
         out_shape=jax.ShapeDtypeStruct((32, 1, LANES), jnp.float32),
-        in_specs=[vmem, vmem, vmem, vmem, vmem],
+        in_specs=[vmem, vmem, vmem],
         out_specs=vmem,
         compiler_params=pltpu.CompilerParams(vmem_limit_bytes=8 * MIB),
-    )(shifted, got, kept, sent, stiff)
+    )(windows, got, fixed)
     planes = [
         [group * strips + plane * PLANE + inner for group in range(groups) for inner in range(PLANE)]
         for plane in range(strips // PLANE)

time: 28.2 us -> 27.9 us (0.989)
  blocking collectives: 14.4 us -> 14.1 us
  transfers between devices with their start and end apart: 3 -> 3, of which waited for: 1 -> 1; matrix products, arithmetic and copies ran while one was open for 0% -> 0% of each run, Pallas kernels for 2% -> 3%
where the time goes in v4:
time: 27.9 us; the launch traced here: 27.7 us
  blocking collectives  14.1 us (51%)
  starting transfers between devices  6.21 us (22%)
  local copies, waits for them, and re-layouts  2.94 us (11%)
  Pallas kernels  2.23 us (8%)
  waiting for transfers between devices  1.5 us (5%)
  between operations  0.66 us (2%)
    all_to_all x1, blocking collectives, on_device(): lax.all_to_all(row, ('gz', 'xy'), 0, 0, axis_index_groups=planes, tiled=T...  14.1 us
    ppermute x1, starting transfers between devices, on_device(): got = lax.ppermute(sections, ('gz', 'xy'), swap)  3.26 us
    unnamed x8, local copies, waits for them, and re-layouts  2.94 us
    ppermute x1, starting transfers between devices, on_device(): beside = lax.ppermute(block, ('gz', 'xy'), hop)  2.17 us
    ppermute x1, waiting for transfers between devices, on_device(): beside = lax.ppermute(block, ('gz', 'xy'), hop)  1.5 us
    pallas_call x1, Pallas kernels, on_device(): pl.pallas_call(relax_kernel, out_shape=(shape, shape), in_specs=[vmem, vm...  1.11 us
    ppermute x1, starting transfers between devices, on_device(): sent = lax.ppermute(peak_offsets, ('gz', 'xy'), fetch)  0.79 us
  transfers between devices with their start and end apart: 3, of which 1 were waited for; matrix products, arithmetic and copies ran while one was open for 0% of the time, Pallas kernels for 3%

profile of v4, /device:TPU:1, one launch (start us, length us, event | category | flops | bytes accessed | tf_op | source)
XLA Modules:
  0.0 27.7 jit_solution(4822154462021851975)
XLA Ops:
  0.6 3.3 %collective-permute-start.1 = (bf16[1,128,1024]{2,1,0:T(8,128)(2,1)}, bf16[1,128,1024]{2,1,0:T(8,128)(2,1)S(1)}, u32[]{:S(2)}, u32[]{:S(2)}) collective-permute-start(bf16[1,128,1024]{2,1,0:T(8,128)(2,1)} %own_ref.1), channel_id=1, source_target_pairs={{0,64},{1,0},{2,66},{3,2},{4,68},{5,4},{6,70},{7,6},{8,72},{9,8},{... | collective-permute-start | bytes 786440 | tf_op jit(solution)/shard_map/ppermute | solution.py:165
  3.9 0.8 %collective-permute-start = (s32[2,1,1,8]{3,2,1,0:T(1,128)}, s32[2,1,1,8]{3,2,1,0:T(1,128)S(1)}, u32[]{:S(2)}, u32[]{:S(2)}) collective-permute-start(s32[2,1,1,8]{3,2,1,0:T(1,128)} %peak_ref.1), channel_id=1, source_target_pairs={{0,2},{1,193},{2,0},{3,195},{4,6},{5,197},{6,4},{7,199},{8,10},{9,... | collective-permute-start | bytes 200 | tf_op jit(solution)/shard_map/ppermute | solution.py:166
  4.7 0.0 copy-start
  4.7 0.9 %copy-done = bf16[1,128,1024]{2,1,0:T(8,128)(2,1)S(1)} copy-done((bf16[1,128,1024]{2,1,0:T(8,128)(2,1)S(1)}, bf16[1,128,1024]{2,1,0:T(8,128)(2,1)}, u32[]{:S(2)}) %copy-start) | copy-done | bytes 262168
  5.6 0.0 copy-start.1
  5.6 0.7 %copy-done.1 = s32[2,1,1,8]{3,2,1,0:T(1,128)S(1)} copy-done((s32[2,1,1,8]{3,2,1,0:T(1,128)S(1)}, s32[2,1,1,8]{3,2,1,0:T(1,128)}, u32[]{:S(2)}) %copy-start.1) | copy-done | bytes 88
  6.3 0.0 copy-start.2
  6.3 0.7 %copy-done.2 = s32[1,1,8]{2,1,0:T(1,128)S(1)} copy-done((s32[1,1,8]{2,1,0:T(1,128)S(1)}, s32[1,1,8]{2,1,0:T(1,128)}, u32[]{:S(2)}) %copy-start.2) | copy-done | bytes 56
  7.0 0.0 copy-start.3
  7.0 0.7 %copy-done.3 = s32[1,1,8]{2,1,0:T(1,128)S(1)} copy-done((s32[1,1,8]{2,1,0:T(1,128)S(1)}, s32[1,1,8]{2,1,0:T(1,128)}, u32[]{:S(2)}) %copy-start.3) | copy-done | bytes 56
  7.6 0.5 %shard_map.59 = (f32[7,8,144,128]{3,2,1,0:T(8,128)S(1)}, f32[1,128]{1,0:T(1,128)S(1)}, s32[2,1,1,8]{3,2,1,0:T(1,128)S(1)}) custom-call(bf16[1,128,1024]{2,1,0:T(8,128)(2,1)S(1)} %copy-done, s32[2,1,1,8]{3,2,1,0:T(1,128)S(1)} %copy-done.1, s32[1,1,8]{2,1,0:T(1,128)S(1)} %copy-done.2, s32[1,1,8]{2,1,0:T(1,128)S(1)} %copy-done.3), custom_call_target="tpu_custom_call" | custom-call | tf_op jit(solution)/shard_map/pallas_call | solution.py:168
  8.1 0.0 collective-permute-done.sent_ref
  8.1 0.3 shard_map.60
  8.4 0.0 collective-permute-done.1.got_ref
  8.4 0.4 %shard_map.61 = f32[32,1,128]{2,1,0:T(1,128)S(1)} custom-call(f32[5,8,128,128]{3,2,1,0:T(8,128)S(1)} %get-tuple-element.10.windows_ref, bf16[1,128,1024]{2,1,0:T(8,128)(2,1)S(1)} %collective-permute-done.1.got_ref, f32[1,128]{1,0:T(1,128)S(1)} %get-tuple-element.11.fixed_ref), custom_call_target="tpu_custom_call" | custom-call | tf_op jit(solution)/shard_map/pallas_call | solution.py:189
  8.8 14.1 %all_to_all.5 = f32[32,1,128]{2,1,0:T(1,128)S(1)} all-to-all(f32[32,1,128]{2,1,0:T(1,128)S(1)} %shard_map.61), channel_id=1, replica_groups={{0,1,2,3,4,5,6,7,64,65,66,67,68,69,70,71,128,129,130,131,132,133,134,13..., dimensions={0} | all-to-all | bytes 32768 | tf_op jit(solution)/shard_map/all_to_all | solution.py:200
  22.9 2.2 %collective-permute-start.2 = (f32[8,128]{1,0:T(8,128)S(1)}, f32[8,128]{1,0:T(8,128)S(1)}, u32[]{:S(2)}, u32[]{:S(2)}) collective-permute-start(f32[8,128]{1,0:T(8,128)S(1)} %bitcast_reduce_fusion.own_ref), channel_id=1, source_target_pairs={{0,9},{1,8},{2,11},{3,10},{4,2},{5,3},{6,0},{7,1},{8,17},{9,16},{1... | collective-permute-start | bytes 12296 | tf_op jit(solution)/shard_map/ppermute | solution.py:202
  25.1 1.5 %collective-permute-done.2.got_ref = f32[8,128]{1,0:T(8,128)S(1)} collective-permute-done((f32[8,128]{1,0:T(8,128)S(1)}, f32[8,128]{1,0:T(8,128)S(1)}, u32[]{:S(2)}, u32[]{:S(2)}) %collective-permute-start.2) | collective-permute-done | bytes 4128 | tf_op jit(solution)/shard_map/ppermute | solution.py:202
  26.6 1.1 %shard_map.62 = (f32[2,1,1,8]{3,2,1,0:T(1,128)}, f32[2,1,1,8]{3,2,1,0:T(1,128)}) custom-call(f32[8,128]{1,0:T(8,128)S(1)} %bitcast_reduce_fusion.own_ref, f32[8,128]{1,0:T(8,128)S(1)} %collective-permute-done.2.got_ref), custom_call_target="tpu_custom_call" | custom-call | tf_op jit(solution)/shard_map/pallas_call | solution.py:204
  (1 shorter events, 0.0 us)
Async XLA Ops:
  0.6 7.8 %collective-permute-start.1 = (bf16[1,128,1024]{2,1,0:T(8,128)(2,1)}, bf16[1,128,1024]{2,1,0:T(8,128)(2,1)S(1)}, u32[]{:S(2)}, u32[]{:S(2)}) collective-permute-start(bf16[1,128,1024]{2,1,0:T(8,128)(2,1)} %own_ref.1), channel_id=1, source_target_pairs={{0,64},{1,0},{2,66},{3,2},{4,68},{5,4},{6,70},{7,6},{8,72},{9,8},{... | collective-permute-start | bytes 786440 | tf_op jit(solution)/shard_map/ppermute | solution.py:165
  3.9 4.2 %collective-permute-start = (s32[2,1,1,8]{3,2,1,0:T(1,128)}, s32[2,1,1,8]{3,2,1,0:T(1,128)S(1)}, u32[]{:S(2)}, u32[]{:S(2)}) collective-permute-start(s32[2,1,1,8]{3,2,1,0:T(1,128)} %peak_ref.1), channel_id=1, source_target_pairs={{0,2},{1,193},{2,0},{3,195},{4,6},{5,197},{6,4},{7,199},{8,10},{9,... | collective-permute-start | bytes 200 | tf_op jit(solution)/shard_map/ppermute | solution.py:166
  4.7 0.9 %copy-start = (bf16[1,128,1024]{2,1,0:T(8,128)(2,1)S(1)}, bf16[1,128,1024]{2,1,0:T(8,128)(2,1)}, u32[]{:S(2)}) copy-start(bf16[1,128,1024]{2,1,0:T(8,128)(2,1)} %own_ref.1) | copy-start | bytes 786436
  5.6 0.7 %copy-start.1 = (s32[2,1,1,8]{3,2,1,0:T(1,128)S(1)}, s32[2,1,1,8]{3,2,1,0:T(1,128)}, u32[]{:S(2)}) copy-start(s32[2,1,1,8]{3,2,1,0:T(1,128)} %peak_ref.1) | copy-start | bytes 196
  6.3 0.7 %copy-start.2 = (s32[1,1,8]{2,1,0:T(1,128)S(1)}, s32[1,1,8]{2,1,0:T(1,128)}, u32[]{:S(2)}) copy-start(s32[1,1,8]{2,1,0:T(1,128)} %conf_ref.1) | copy-start | bytes 100
  7.0 0.7 %copy-start.3 = (s32[1,1,8]{2,1,0:T(1,128)S(1)}, s32[1,1,8]{2,1,0:T(1,128)}, u32[]{:S(2)}) copy-start(s32[1,1,8]{2,1,0:T(1,128)} %mask_ref.1) | copy-start | bytes 100
  22.9 3.7 %collective-permute-start.2 = (f32[8,128]{1,0:T(8,128)S(1)}, f32[8,128]{1,0:T(8,128)S(1)}, u32[]{:S(2)}, u32[]{:S(2)}) collective-permute-start(f32[8,128]{1,0:T(8,128)S(1)} %bitcast_reduce_fusion.own_ref), channel_id=1, source_target_pairs={{0,9},{1,8},{2,11},{3,10},{4,2},{5,3},{6,0},{7,1},{8,17},{9,16},{1... | collective-permute-start | bytes 12296 | tf_op jit(solution)/shard_map/ppermute | solution.py:202

commit v5 on v4

--- a/solution.py
+++ b/solution.py
@@ -50,10 +50,10 @@
         right = REACH + sign * peaks[1][0, j]
         for k, (u, v) in enumerate(((0, 0), (1, 0), (-1, 0), (0, 1), (0, -1))):
             windows_ref[k, j] = shifted_ref[right + v, j, pl.ds(down + u, PATCH), :]
-    gap = jnp.zeros((1, LANES - 2 * COLS), jnp.float32)
-    flow = [peaks[0].astype(jnp.float32), peaks[1].astype(jnp.float32), gap]
-    flow = jnp.concatenate(flow, axis=1)
-    fixed_ref[...] = stiff_ref[...] + pltpu.roll(flow, target * 16, 1)
+    flow = [peaks[0].astype(jnp.float32), peaks[1].astype(jnp.float32)] * 4
+    flow = jnp.concatenate(flow + [jnp.zeros((1, LANES // 2), jnp.float32)], axis=1)
+    lane = lax.broadcasted_iota(jnp.int32, (1, LANES), 1)
+    fixed_ref[...] = stiff_ref[...] + jnp.where(lane >= target * 16, flow, 0.0)
 
 
 def correlate_kernel(windows_ref, got_ref, fixed_ref, out_ref):
@@ -84,8 +84,10 @@
     delta_x = scale * (x_plus - x_minus) / (jnp.abs(x_minus) + jnp.abs(center) + jnp.abs(x_plus) + 1.0)
     lane = lax.broadcasted_iota(jnp.int32, (COLS, LANES), 1)
     patch = lax.broadcasted_iota(jnp.int32, (COLS, LANES), 0)
-    spread = jnp.where(lane == target * 16 + patch, delta_y, 0.0)
-    spread = spread + jnp.where(lane == target * 16 + COLS + patch, delta_x, 0.0)
+    later = jnp.logical_and(lane >= target * 16, lane < 64)
+    spread = jnp.where(lax.rem(lane, 16) == patch, delta_y, 0.0)
+    spread = spread + jnp.where(lax.rem(lane, 16) == COLS + patch, delta_x, 0.0)
+    spread = jnp.where(later, spread, 0.0)
     row = fixed_ref[...] + jnp.sum(spread, axis=0, keepdims=True)
     out_ref[...] = jnp.broadcast_to(row[None], out_ref.shape)
 
@@ -110,26 +112,26 @@
     has_down = row < 63
     has_left = col > 0
     has_right = col < COLS - 1
-    flow = jnp.where(lane < 64, window, 0.0)
-    stiff = jnp.where(lane < 64, pltpu.roll(window, 64, 1), 0.0)
-    next_stiff = jnp.where(lane < 48, pltpu.roll(window, 48, 1), 0.0)
-    next_flow = jnp.where(lane < 48, pltpu.roll(window, LANES - 16, 1), 0.0)
-    start = flow + jnp.where(lane >= 16, pltpu.roll(flow, 16, 1), 0.0)
-    start = start + (
-        jnp.where(lane >= 32, pltpu.roll(flow, 32, 1), 0.0)
-        + jnp.where(lane >= 48, pltpu.roll(flow, 48, 1), 0.0)
-    )
-    nodes = start
-    for _ in range(ITERS):
-        rows = jnp.where(has_up, pltpu.roll(nodes, 1, 0) - nodes, 0.0)
-        rows = rows + jnp.where(has_down, pltpu.roll(nodes, 2 * PLANE - 1, 0) - nodes, 0.0)
-        cols = jnp.where(has_left, pltpu.roll(nodes, 1, 1) - nodes, 0.0)
-        cols = cols + jnp.where(has_right, pltpu.roll(nodes, LANES - 1, 1) - nodes, 0.0)
-        links = stiff * (pltpu.roll(nodes, 16, 1) + flow - nodes)
-        links = links + next_stiff * (pltpu.roll(nodes, LANES - 16, 1) - next_flow - nodes)
-        nodes = nodes + STEP_SIZE * ((rows + cols) + links)
+    start = jnp.where(lane < 64, window, 0.0)
+    stiff = STEP_SIZE * jnp.where(lane < 64, pltpu.roll(window, 64, 1), 0.0)
+    next_stiff = STEP_SIZE * jnp.where(lane < 48, pltpu.roll(window, 48, 1), 0.0)
+    flow = start - jnp.where(lane >= 16, pltpu.roll(start, 16, 1), 0.0)
+
+    def neighbours(values):
+        rows = jnp.where(has_up, pltpu.roll(values, 1, 0) - values, 0.0)
+        rows = rows + jnp.where(has_down, pltpu.roll(values, 2 * PLANE - 1, 0) - values, 0.0)
+        cols = jnp.where(has_left, pltpu.roll(values, 1, 1) - values, 0.0)
+        cols = cols + jnp.where(has_right, pltpu.roll(values, LANES - 1, 1) - values, 0.0)
+        return STEP_SIZE * (rows + cols)
+
+    first = neighbours(start)
+    moved = first
+    for _ in range(ITERS - 1):
+        links = stiff * (pltpu.roll(moved, 16, 1) - moved)
+        links = links + next_stiff * (pltpu.roll(moved, LANES - 16, 1) - moved)
+        moved = (moved + first) + (neighbours(moved) + links)
     turn = lax.rem(LANES - gz * 16, LANES)
-    for value, ref in ((flow, flow_ref), (nodes - start, corr_ref)):
+    for value, ref in ((flow, flow_ref), (moved, corr_ref)):
         mine = jnp.sum(jnp.where(local == here, value, 0.0), axis=0, keepdims=True)
         mine = pltpu.roll(mine, turn, 1)
         ref[0, 0] = mine[:, 0:COLS]

time: 27.9 us -> 27.8 us (level)
  no operation moved by 1% of the time
where the time goes in v5:
time: 27.8 us; the launch traced here: 27.6 us
  blocking collectives  14.1 us (51%)
  starting transfers between devices  6.21 us (22%)
  local copies, waits for them, and re-layouts  2.94 us (11%)
  Pallas kernels  2.15 us (8%)
  waiting for transfers between devices  1.5 us (5%)
  between operations  0.66 us (2%)
    all_to_all x1, blocking collectives, on_device(): lax.all_to_all(row, ('gz', 'xy'), 0, 0, axis_index_groups=planes, tiled=T...  14.1 us
    ppermute x1, starting transfers between devices, on_device(): got = lax.ppermute(sections, ('gz', 'xy'), swap)  3.26 us
    unnamed x8, local copies, waits for them, and re-layouts  2.94 us
    ppermute x1, starting transfers between devices, on_device(): beside = lax.ppermute(block, ('gz', 'xy'), hop)  2.17 us
    ppermute x1, waiting for transfers between devices, on_device(): beside = lax.ppermute(block, ('gz', 'xy'), hop)  1.5 us
    pallas_call x1, Pallas kernels, on_device(): pl.pallas_call(relax_kernel, out_shape=(shape, shape), in_specs=[vmem, vm...  1.02 us
    ppermute x1, starting transfers between devices, on_device(): sent = lax.ppermute(peak_offsets, ('gz', 'xy'), fetch)  0.79 us
  transfers between devices with their start and end apart: 3, of which 1 were waited for; matrix products, arithmetic and copies ran while one was open for 0% of the time, Pallas kernels for 3%

profile of v5, /device:TPU:1, one launch (start us, length us, event | category | flops | bytes accessed | tf_op | source)
XLA Modules:
  0.0 27.6 jit_solution(895748730333507172)
XLA Ops:
  0.6 3.3 %collective-permute-start.1 = (bf16[1,128,1024]{2,1,0:T(8,128)(2,1)}, bf16[1,128,1024]{2,1,0:T(8,128)(2,1)S(1)}, u32[]{:S(2)}, u32[]{:S(2)}) collective-permute-start(bf16[1,128,1024]{2,1,0:T(8,128)(2,1)} %own_ref.1), channel_id=1, source_target_pairs={{0,64},{1,0},{2,66},{3,2},{4,68},{5,4},{6,70},{7,6},{8,72},{9,8},{... | collective-permute-start | bytes 786440 | tf_op jit(solution)/shard_map/ppermute | solution.py:167
  3.9 0.8 %collective-permute-start = (s32[2,1,1,8]{3,2,1,0:T(1,128)}, s32[2,1,1,8]{3,2,1,0:T(1,128)S(1)}, u32[]{:S(2)}, u32[]{:S(2)}) collective-permute-start(s32[2,1,1,8]{3,2,1,0:T(1,128)} %peak_ref.1), channel_id=1, source_target_pairs={{0,2},{1,193},{2,0},{3,195},{4,6},{5,197},{6,4},{7,199},{8,10},{9,... | collective-permute-start | bytes 200 | tf_op jit(solution)/shard_map/ppermute | solution.py:168
  4.7 0.0 copy-start
  4.7 0.9 %copy-done = bf16[1,128,1024]{2,1,0:T(8,128)(2,1)S(1)} copy-done((bf16[1,128,1024]{2,1,0:T(8,128)(2,1)S(1)}, bf16[1,128,1024]{2,1,0:T(8,128)(2,1)}, u32[]{:S(2)}) %copy-start) | copy-done | bytes 262168
  5.6 0.0 copy-start.1
  5.6 0.7 %copy-done.1 = s32[2,1,1,8]{3,2,1,0:T(1,128)S(1)} copy-done((s32[2,1,1,8]{3,2,1,0:T(1,128)S(1)}, s32[2,1,1,8]{3,2,1,0:T(1,128)}, u32[]{:S(2)}) %copy-start.1) | copy-done | bytes 88
  6.3 0.0 copy-start.2
  6.3 0.7 %copy-done.2 = s32[1,1,8]{2,1,0:T(1,128)S(1)} copy-done((s32[1,1,8]{2,1,0:T(1,128)S(1)}, s32[1,1,8]{2,1,0:T(1,128)}, u32[]{:S(2)}) %copy-start.2) | copy-done | bytes 56
  7.0 0.0 copy-start.3
  7.0 0.7 %copy-done.3 = s32[1,1,8]{2,1,0:T(1,128)S(1)} copy-done((s32[1,1,8]{2,1,0:T(1,128)S(1)}, s32[1,1,8]{2,1,0:T(1,128)}, u32[]{:S(2)}) %copy-start.3) | copy-done | bytes 56
  7.6 0.5 %shard_map.59 = (f32[7,8,144,128]{3,2,1,0:T(8,128)S(1)}, f32[1,128]{1,0:T(1,128)S(1)}, s32[2,1,1,8]{3,2,1,0:T(1,128)S(1)}) custom-call(bf16[1,128,1024]{2,1,0:T(8,128)(2,1)S(1)} %copy-done, s32[2,1,1,8]{3,2,1,0:T(1,128)S(1)} %copy-done.1, s32[1,1,8]{2,1,0:T(1,128)S(1)} %copy-done.2, s32[1,1,8]{2,1,0:T(1,128)S(1)} %copy-done.3), custom_call_target="tpu_custom_call" | custom-call | tf_op jit(solution)/shard_map/pallas_call | solution.py:170
  8.1 0.0 collective-permute-done.sent_ref
  8.1 0.3 shard_map.60
  8.4 0.0 collective-permute-done.1.got_ref
  8.4 0.4 %shard_map.61 = f32[32,1,128]{2,1,0:T(1,128)S(1)} custom-call(f32[5,8,128,128]{3,2,1,0:T(8,128)S(1)} %get-tuple-element.10.windows_ref, bf16[1,128,1024]{2,1,0:T(8,128)(2,1)S(1)} %collective-permute-done.1.got_ref, f32[1,128]{1,0:T(1,128)S(1)} %get-tuple-element.11.fixed_ref), custom_call_target="tpu_custom_call" | custom-call | tf_op jit(solution)/shard_map/pallas_call | solution.py:191
  8.8 14.1 %all_to_all.5 = f32[32,1,128]{2,1,0:T(1,128)S(1)} all-to-all(f32[32,1,128]{2,1,0:T(1,128)S(1)} %shard_map.61), channel_id=1, replica_groups={{0,1,2,3,4,5,6,7,64,65,66,67,68,69,70,71,128,129,130,131,132,133,134,13..., dimensions={0} | all-to-all | bytes 32768 | tf_op jit(solution)/shard_map/all_to_all | solution.py:202
  22.9 2.2 %collective-permute-start.2 = (f32[8,128]{1,0:T(8,128)S(1)}, f32[8,128]{1,0:T(8,128)S(1)}, u32[]{:S(2)}, u32[]{:S(2)}) collective-permute-start(f32[8,128]{1,0:T(8,128)S(1)} %bitcast_reduce_fusion.own_ref), channel_id=1, source_target_pairs={{0,9},{1,8},{2,11},{3,10},{4,2},{5,3},{6,0},{7,1},{8,17},{9,16},{1... | collective-permute-start | bytes 12296 | tf_op jit(solution)/shard_map/ppermute | solution.py:204
  25.1 1.5 %collective-permute-done.2.got_ref = f32[8,128]{1,0:T(8,128)S(1)} collective-permute-done((f32[8,128]{1,0:T(8,128)S(1)}, f32[8,128]{1,0:T(8,128)S(1)}, u32[]{:S(2)}, u32[]{:S(2)}) %collective-permute-start.2) | collective-permute-done | bytes 4128 | tf_op jit(solution)/shard_map/ppermute | solution.py:204
  26.6 1.0 %shard_map.62 = (f32[2,1,1,8]{3,2,1,0:T(1,128)}, f32[2,1,1,8]{3,2,1,0:T(1,128)}) custom-call(f32[8,128]{1,0:T(8,128)S(1)} %bitcast_reduce_fusion.own_ref, f32[8,128]{1,0:T(8,128)S(1)} %collective-permute-done.2.got_ref), custom_call_target="tpu_custom_call" | custom-call | tf_op jit(solution)/shard_map/pallas_call | solution.py:206
  (1 shorter events, 0.0 us)
Async XLA Ops:
  0.6 7.8 %collective-permute-start.1 = (bf16[1,128,1024]{2,1,0:T(8,128)(2,1)}, bf16[1,128,1024]{2,1,0:T(8,128)(2,1)S(1)}, u32[]{:S(2)}, u32[]{:S(2)}) collective-permute-start(bf16[1,128,1024]{2,1,0:T(8,128)(2,1)} %own_ref.1), channel_id=1, source_target_pairs={{0,64},{1,0},{2,66},{3,2},{4,68},{5,4},{6,70},{7,6},{8,72},{9,8},{... | collective-permute-start | bytes 786440 | tf_op jit(solution)/shard_map/ppermute | solution.py:167
  3.9 4.2 %collective-permute-start = (s32[2,1,1,8]{3,2,1,0:T(1,128)}, s32[2,1,1,8]{3,2,1,0:T(1,128)S(1)}, u32[]{:S(2)}, u32[]{:S(2)}) collective-permute-start(s32[2,1,1,8]{3,2,1,0:T(1,128)} %peak_ref.1), channel_id=1, source_target_pairs={{0,2},{1,193},{2,0},{3,195},{4,6},{5,197},{6,4},{7,199},{8,10},{9,... | collective-permute-start | bytes 200 | tf_op jit(solution)/shard_map/ppermute | solution.py:168
  4.7 0.9 %copy-start = (bf16[1,128,1024]{2,1,0:T(8,128)(2,1)S(1)}, bf16[1,128,1024]{2,1,0:T(8,128)(2,1)}, u32[]{:S(2)}) copy-start(bf16[1,128,1024]{2,1,0:T(8,128)(2,1)} %own_ref.1) | copy-start | bytes 786436
  5.6 0.7 %copy-start.1 = (s32[2,1,1,8]{3,2,1,0:T(1,128)S(1)}, s32[2,1,1,8]{3,2,1,0:T(1,128)}, u32[]{:S(2)}) copy-start(s32[2,1,1,8]{3,2,1,0:T(1,128)} %peak_ref.1) | copy-start | bytes 196
  6.3 0.7 %copy-start.2 = (s32[1,1,8]{2,1,0:T(1,128)S(1)}, s32[1,1,8]{2,1,0:T(1,128)}, u32[]{:S(2)}) copy-start(s32[1,1,8]{2,1,0:T(1,128)} %conf_ref.1) | copy-start | bytes 100
  7.0 0.7 %copy-start.3 = (s32[1,1,8]{2,1,0:T(1,128)S(1)}, s32[1,1,8]{2,1,0:T(1,128)}, u32[]{:S(2)}) copy-start(s32[1,1,8]{2,1,0:T(1,128)} %mask_ref.1) | copy-start | bytes 100
  22.9 3.7 %collective-permute-start.2 = (f32[8,128]{1,0:T(8,128)S(1)}, f32[8,128]{1,0:T(8,128)S(1)}, u32[]{:S(2)}, u32[]{:S(2)}) collective-permute-start(f32[8,128]{1,0:T(8,128)S(1)} %bitcast_reduce_fusion.own_ref), channel_id=1, source_target_pairs={{0,9},{1,8},{2,11},{3,10},{4,2},{5,3},{6,0},{7,1},{8,17},{9,16},{1... | collective-permute-start | bytes 12296 | tf_op jit(solution)/shard_map/ppermute | solution.py:204

commit v6 on v5

--- a/solution.py
+++ b/solution.py
@@ -92,7 +92,23 @@
     out_ref[...] = jnp.broadcast_to(row[None], out_ref.shape)
 
 
-def relax_kernel(own_ref, got_ref, flow_ref, corr_ref):
+def put_row(value, hit, turn, ref):
+    mine = jnp.sum(jnp.where(hit, value, 0.0), axis=0, keepdims=True)
+    mine = pltpu.roll(mine, turn, 1)
+    ref[0, 0] = mine[:, 0:COLS]
+    ref[1, 0] = mine[:, COLS : 2 * COLS]
+
+
+def flow_kernel(own_ref, flow_ref):
+    gz, xy = place()
+    lane = lax.broadcasted_iota(jnp.int32, (PLANE, LANES), 1)
+    row = lax.broadcasted_iota(jnp.int32, (PLANE, LANES), 0)
+    start = own_ref[...]
+    flow = start - jnp.where(lane >= 16, pltpu.roll(start, 16, 1), 0.0)
+    put_row(flow, row == lax.rem(xy, PLANE), lax.rem(LANES - gz * 16, LANES), flow_ref)
+
+
+def relax_kernel(own_ref, got_ref, corr_ref):
     gz, xy = place()
     z = xy // PLANE
     inner = lax.rem(xy, PLANE)
@@ -115,7 +131,6 @@
     start = jnp.where(lane < 64, window, 0.0)
     stiff = STEP_SIZE * jnp.where(lane < 64, pltpu.roll(window, 64, 1), 0.0)
     next_stiff = STEP_SIZE * jnp.where(lane < 48, pltpu.roll(window, 48, 1), 0.0)
-    flow = start - jnp.where(lane >= 16, pltpu.roll(start, 16, 1), 0.0)
 
     def neighbours(values):
         rows = jnp.where(has_up, pltpu.roll(values, 1, 0) - values, 0.0)
@@ -130,12 +145,7 @@
         links = stiff * (pltpu.roll(moved, 16, 1) - moved)
         links = links + next_stiff * (pltpu.roll(moved, LANES - 16, 1) - moved)
         moved = (moved + first) + (neighbours(moved) + links)
-    turn = lax.rem(LANES - gz * 16, LANES)
-    for value, ref in ((flow, flow_ref), (moved, corr_ref)):
-        mine = jnp.sum(jnp.where(local == here, value, 0.0), axis=0, keepdims=True)
-        mine = pltpu.roll(mine, turn, 1)
-        ref[0, 0] = mine[:, 0:COLS]
-        ref[1, 0] = mine[:, COLS : 2 * COLS]
+    put_row(moved, local == here, lax.rem(LANES - gz * 16, LANES), corr_ref)
 
 
 def routes(groups, strips):
@@ -203,13 +213,21 @@
     block = jnp.sum(block.reshape(groups, PLANE, LANES), axis=0)
     beside = lax.ppermute(block, ("gz", "xy"), hop)
     shape = jax.ShapeDtypeStruct(peak_offsets.shape, jnp.float32)
-    return pl.pallas_call(
+    flow = pl.pallas_call(
+        flow_kernel,
+        out_shape=shape,
+        in_specs=[vmem],
+        out_specs=vmem,
+        compiler_params=pltpu.CompilerParams(vmem_limit_bytes=4 * MIB),
+    )(block)
+    correction = pl.pallas_call(
         relax_kernel,
-        out_shape=(shape, shape),
+        out_shape=shape,
         in_specs=[vmem, vmem],
-        out_specs=(vmem, vmem),
+        out_specs=vmem,
         compiler_params=pltpu.CompilerParams(vmem_limit_bytes=4 * MIB),
     )(block, beside)
+    return flow, correction
 
 
 def solution(mesh):

time: 27.8 us -> 27.8 us (level)
  Pallas kernels: 2.15 us -> 2.92 us
  waiting for transfers between devices: 1.5 us -> 0.73 us
    ppermute x1, waiting for transfers between devices: 1.5 us -> 0.72 us  [on_device(): beside = lax.ppermute(block, ('gz', 'xy'), hop)]
    pallas_call x1 -> x2, Pallas kernels: 1.02 us -> 1.79 us  [the longest x1 1.02 us: on_device(): pl.pallas_call(relax_kernel, out_shape=shape, in_specs=[vmem, vmem], out_...]
  transfers between devices with their start and end apart: 3 -> 3, of which waited for: 1 -> 1; matrix products, arithmetic and copies ran while one was open for 0% -> 0% of each run, Pallas kernels for 3% -> 6%
where the time goes in v6:
time: 27.8 us; the launch traced here: 27.6 us
  blocking collectives  14.1 us (51%)
  starting transfers between devices  6.21 us (22%)
  local copies, waits for them, and re-layouts  2.94 us (11%)
  Pallas kernels  2.92 us (11%)
  waiting for transfers between devices  0.73 us (3%)
  between operations  0.66 us (2%)
    all_to_all x1, blocking collectives, on_device(): lax.all_to_all(row, ('gz', 'xy'), 0, 0, axis_index_groups=planes, tiled=T...  14.1 us
    ppermute x1, starting transfers between devices, on_device(): got = lax.ppermute(sections, ('gz', 'xy'), swap)  3.26 us
    unnamed x8, local copies, waits for them, and re-layouts  2.94 us
    ppermute x1, starting transfers between devices, on_device(): beside = lax.ppermute(block, ('gz', 'xy'), hop)  2.17 us
    pallas_call x1, Pallas kernels, on_device(): pl.pallas_call(relax_kernel, out_shape=shape, in_specs=[vmem, vmem], out_...  1.02 us
    ppermute x1, starting transfers between devices, on_device(): sent = lax.ppermute(peak_offsets, ('gz', 'xy'), fetch)  0.79 us
    pallas_call x1, Pallas kernels, on_device(): pl.pallas_call(flow_kernel, out_shape=shape, in_specs=[vmem], out_specs=v...  0.77 us
    ppermute x1, waiting for transfers between devices, on_device(): beside = lax.ppermute(block, ('gz', 'xy'), hop)  0.72 us
  transfers between devices with their start and end apart: 3, of which 1 were waited for; matrix products, arithmetic and copies ran while one was open for 0% of the time, Pallas kernels for 6%

profile of v6, /device:TPU:1, one launch (start us, length us, event | category | flops | bytes accessed | tf_op | source)
XLA Modules:
  0.0 27.6 jit_solution(11325034394850753705)
XLA Ops:
  0.6 3.3 %collective-permute-start.1 = (bf16[1,128,1024]{2,1,0:T(8,128)(2,1)}, bf16[1,128,1024]{2,1,0:T(8,128)(2,1)S(1)}, u32[]{:S(2)}, u32[]{:S(2)}) collective-permute-start(bf16[1,128,1024]{2,1,0:T(8,128)(2,1)} %own_ref.1), channel_id=1, source_target_pairs={{0,64},{1,0},{2,66},{3,2},{4,68},{5,4},{6,70},{7,6},{8,72},{9,8},{... | collective-permute-start | bytes 786440 | tf_op jit(solution)/shard_map/ppermute | solution.py:177
  3.9 0.8 %collective-permute-start = (s32[2,1,1,8]{3,2,1,0:T(1,128)}, s32[2,1,1,8]{3,2,1,0:T(1,128)S(1)}, u32[]{:S(2)}, u32[]{:S(2)}) collective-permute-start(s32[2,1,1,8]{3,2,1,0:T(1,128)} %peak_ref.1), channel_id=1, source_target_pairs={{0,2},{1,193},{2,0},{3,195},{4,6},{5,197},{6,4},{7,199},{8,10},{9,... | collective-permute-start | bytes 200 | tf_op jit(solution)/shard_map/ppermute | solution.py:178
  4.7 0.0 copy-start
  4.7 0.9 %copy-done = bf16[1,128,1024]{2,1,0:T(8,128)(2,1)S(1)} copy-done((bf16[1,128,1024]{2,1,0:T(8,128)(2,1)S(1)}, bf16[1,128,1024]{2,1,0:T(8,128)(2,1)}, u32[]{:S(2)}) %copy-start) | copy-done | bytes 262168
  5.6 0.0 copy-start.1
  5.6 0.7 %copy-done.1 = s32[2,1,1,8]{3,2,1,0:T(1,128)S(1)} copy-done((s32[2,1,1,8]{3,2,1,0:T(1,128)S(1)}, s32[2,1,1,8]{3,2,1,0:T(1,128)}, u32[]{:S(2)}) %copy-start.1) | copy-done | bytes 88
  6.3 0.0 copy-start.2
  6.3 0.7 %copy-done.2 = s32[1,1,8]{2,1,0:T(1,128)S(1)} copy-done((s32[1,1,8]{2,1,0:T(1,128)S(1)}, s32[1,1,8]{2,1,0:T(1,128)}, u32[]{:S(2)}) %copy-start.2) | copy-done | bytes 56
  7.0 0.0 copy-start.3
  7.0 0.7 %copy-done.3 = s32[1,1,8]{2,1,0:T(1,128)S(1)} copy-done((s32[1,1,8]{2,1,0:T(1,128)S(1)}, s32[1,1,8]{2,1,0:T(1,128)}, u32[]{:S(2)}) %copy-start.3) | copy-done | bytes 56
  7.6 0.5 %shard_map.59 = (f32[7,8,144,128]{3,2,1,0:T(8,128)S(1)}, f32[1,128]{1,0:T(1,128)S(1)}, s32[2,1,1,8]{3,2,1,0:T(1,128)S(1)}) custom-call(bf16[1,128,1024]{2,1,0:T(8,128)(2,1)S(1)} %copy-done, s32[2,1,1,8]{3,2,1,0:T(1,128)S(1)} %copy-done.1, s32[1,1,8]{2,1,0:T(1,128)S(1)} %copy-done.2, s32[1,1,8]{2,1,0:T(1,128)S(1)} %copy-done.3), custom_call_target="tpu_custom_call" | custom-call | tf_op jit(solution)/shard_map/pallas_call | solution.py:180
  8.1 0.0 collective-permute-done.sent_ref
  8.1 0.3 shard_map.60
  8.4 0.0 collective-permute-done.1.got_ref
  8.4 0.4 %shard_map.61 = f32[32,1,128]{2,1,0:T(1,128)S(1)} custom-call(f32[5,8,128,128]{3,2,1,0:T(8,128)S(1)} %get-tuple-element.10.windows_ref, bf16[1,128,1024]{2,1,0:T(8,128)(2,1)S(1)} %collective-permute-done.1.got_ref, f32[1,128]{1,0:T(1,128)S(1)} %get-tuple-element.11.fixed_ref), custom_call_target="tpu_custom_call" | custom-call | tf_op jit(solution)/shard_map/pallas_call | solution.py:201
  8.8 14.1 %all_to_all.5 = f32[32,1,128]{2,1,0:T(1,128)S(1)} all-to-all(f32[32,1,128]{2,1,0:T(1,128)S(1)} %shard_map.61), channel_id=1, replica_groups={{0,1,2,3,4,5,6,7,64,65,66,67,68,69,70,71,128,129,130,131,132,133,134,13..., dimensions={0} | all-to-all | bytes 32768 | tf_op jit(solution)/shard_map/all_to_all | solution.py:212
  22.9 2.2 %collective-permute-start.2 = (f32[8,128]{1,0:T(8,128)S(1)}, f32[8,128]{1,0:T(8,128)S(1)}, u32[]{:S(2)}, u32[]{:S(2)}) collective-permute-start(f32[8,128]{1,0:T(8,128)S(1)} %bitcast_reduce_fusion.own_ref), channel_id=1, source_target_pairs={{0,9},{1,8},{2,11},{3,10},{4,2},{5,3},{6,0},{7,1},{8,17},{9,16},{1... | collective-permute-start | bytes 12296 | tf_op jit(solution)/shard_map/ppermute | solution.py:214
  25.1 0.8 %shard_map.62 = f32[2,1,1,8]{3,2,1,0:T(1,128)} custom-call(f32[8,128]{1,0:T(8,128)S(1)} %bitcast_reduce_fusion.own_ref), custom_call_target="tpu_custom_call" | custom-call | tf_op jit(solution)/shard_map/pallas_call | solution.py:216
  25.9 0.7 %collective-permute-done.2.got_ref = f32[8,128]{1,0:T(8,128)S(1)} collective-permute-done((f32[8,128]{1,0:T(8,128)S(1)}, f32[8,128]{1,0:T(8,128)S(1)}, u32[]{:S(2)}, u32[]{:S(2)}) %collective-permute-start.2) | collective-permute-done | bytes 4128 | tf_op jit(solution)/shard_map/ppermute | solution.py:214
  26.6 1.0 %shard_map.63 = f32[2,1,1,8]{3,2,1,0:T(1,128)} custom-call(f32[8,128]{1,0:T(8,128)S(1)} %bitcast_reduce_fusion.own_ref, f32[8,128]{1,0:T(8,128)S(1)} %collective-permute-done.2.got_ref), custom_call_target="tpu_custom_call" | custom-call | tf_op jit(solution)/shard_map/pallas_call | solution.py:223
  (1 shorter events, 0.0 us)
Async XLA Ops:
  0.6 7.8 %collective-permute-start.1 = (bf16[1,128,1024]{2,1,0:T(8,128)(2,1)}, bf16[1,128,1024]{2,1,0:T(8,128)(2,1)S(1)}, u32[]{:S(2)}, u32[]{:S(2)}) collective-permute-start(bf16[1,128,1024]{2,1,0:T(8,128)(2,1)} %own_ref.1), channel_id=1, source_target_pairs={{0,64},{1,0},{2,66},{3,2},{4,68},{5,4},{6,70},{7,6},{8,72},{9,8},{... | collective-permute-start | bytes 786440 | tf_op jit(solution)/shard_map/ppermute | solution.py:177
  3.9 4.2 %collective-permute-start = (s32[2,1,1,8]{3,2,1,0:T(1,128)}, s32[2,1,1,8]{3,2,1,0:T(1,128)S(1)}, u32[]{:S(2)}, u32[]{:S(2)}) collective-permute-start(s32[2,1,1,8]{3,2,1,0:T(1,128)} %peak_ref.1), channel_id=1, source_target_pairs={{0,2},{1,193},{2,0},{3,195},{4,6},{5,197},{6,4},{7,199},{8,10},{9,... | collective-permute-start | bytes 200 | tf_op jit(solution)/shard_map/ppermute | solution.py:178
  4.7 0.9 %copy-start = (bf16[1,128,1024]{2,1,0:T(8,128)(2,1)S(1)}, bf16[1,128,1024]{2,1,0:T(8,128)(2,1)}, u32[]{:S(2)}) copy-start(bf16[1,128,1024]{2,1,0:T(8,128)(2,1)} %own_ref.1) | copy-start | bytes 786436
  5.6 0.7 %copy-start.1 = (s32[2,1,1,8]{3,2,1,0:T(1,128)S(1)}, s32[2,1,1,8]{3,2,1,0:T(1,128)}, u32[]{:S(2)}) copy-start(s32[2,1,1,8]{3,2,1,0:T(1,128)} %peak_ref.1) | copy-start | bytes 196
  6.3 0.7 %copy-start.2 = (s32[1,1,8]{2,1,0:T(1,128)S(1)}, s32[1,1,8]{2,1,0:T(1,128)}, u32[]{:S(2)}) copy-start(s32[1,1,8]{2,1,0:T(1,128)} %conf_ref.1) | copy-start | bytes 100
  7.0 0.7 %copy-start.3 = (s32[1,1,8]{2,1,0:T(1,128)S(1)}, s32[1,1,8]{2,1,0:T(1,128)}, u32[]{:S(2)}) copy-start(s32[1,1,8]{2,1,0:T(1,128)} %mask_ref.1) | copy-start | bytes 100
  22.9 3.7 %collective-permute-start.2 = (f32[8,128]{1,0:T(8,128)S(1)}, f32[8,128]{1,0:T(8,128)S(1)}, u32[]{:S(2)}, u32[]{:S(2)}) collective-permute-start(f32[8,128]{1,0:T(8,128)S(1)} %bitcast_reduce_fusion.own_ref), channel_id=1, source_target_pairs={{0,9},{1,8},{2,11},{3,10},{4,2},{5,3},{6,0},{7,1},{8,17},{9,16},{1... | collective-permute-start | bytes 12296 | tf_op jit(solution)/shard_map/ppermute | solution.py:214

commit v7 on v6

--- a/solution.py
+++ b/solution.py
@@ -92,20 +92,18 @@
     out_ref[...] = jnp.broadcast_to(row[None], out_ref.shape)
 
 
-def put_row(value, hit, turn, ref):
-    mine = jnp.sum(jnp.where(hit, value, 0.0), axis=0, keepdims=True)
-    mine = pltpu.roll(mine, turn, 1)
-    ref[0, 0] = mine[:, 0:COLS]
-    ref[1, 0] = mine[:, COLS : 2 * COLS]
+def put_row(value, index, lanes, ref):
+    mine = pltpu.roll(value, lax.rem(PLANE - index, PLANE), 0)[0:1]
+    ref[0, 0] = pltpu.roll(mine, lax.rem(LANES - lanes, LANES), 1)[:, 0:COLS]
+    ref[1, 0] = pltpu.roll(mine, LANES - COLS - lanes, 1)[:, 0:COLS]
 
 
 def flow_kernel(own_ref, flow_ref):
     gz, xy = place()
     lane = lax.broadcasted_iota(jnp.int32, (PLANE, LANES), 1)
-    row = lax.broadcasted_iota(jnp.int32, (PLANE, LANES), 0)
     start = own_ref[...]
     flow = start - jnp.where(lane >= 16, pltpu.roll(start, 16, 1), 0.0)
-    put_row(flow, row == lax.rem(xy, PLANE), lax.rem(LANES - gz * 16, LANES), flow_ref)
+    put_row(flow, lax.rem(xy, PLANE), gz * 16, flow_ref)
 
 
 def relax_kernel(own_ref, got_ref, corr_ref):
@@ -118,7 +116,6 @@
     got = got_ref[...]
     window = jnp.concatenate([jnp.where(upper, got, own), jnp.where(upper, own, got)], axis=0)
     base = jnp.where(upper, z - 1, z) * PLANE
-    here = jnp.where(upper, PLANE + inner, inner)
     shape = (2 * PLANE, LANES)
     lane = lax.broadcasted_iota(jnp.int32, shape, 1)
     local = lax.broadcasted_iota(jnp.int32, shape, 0)
@@ -145,7 +142,7 @@
         links = stiff * (pltpu.roll(moved, 16, 1) - moved)
         links = links + next_stiff * (pltpu.roll(moved, LANES - 16, 1) - moved)
         moved = (moved + first) + (neighbours(moved) + links)
-    put_row(moved, local == here, lax.rem(LANES - gz * 16, LANES), corr_ref)
+    put_row(jnp.where(upper, moved[PLANE:], moved[:PLANE]), inner, gz * 16, corr_ref)
 
 
 def routes(groups, strips):

time: 27.8 us -> 27.7 us (level)
  transfers between devices with their start and end apart: 3 -> 3, of which waited for: 1 -> 1; matrix products, arithmetic and copies ran while one was open for 0% -> 0% of each run, Pallas kernels for 6% -> 5%
where the time goes in v7:
time: 27.7 us; the launch traced here: 27.5 us
  blocking collectives  14.1 us (51%)
  starting transfers between devices  6.21 us (22%)
  local copies, waits for them, and re-layouts  2.94 us (11%)
  Pallas kernels  2.78 us (10%)
  waiting for transfers between devices  0.8 us (3%)
  between operations  0.66 us (2%)
    all_to_all x1, blocking collectives, on_device(): lax.all_to_all(row, ('gz', 'xy'), 0, 0, axis_index_groups=planes, tiled=T...  14.1 us
    ppermute x1, starting transfers between devices, on_device(): got = lax.ppermute(sections, ('gz', 'xy'), swap)  3.26 us
    unnamed x8, local copies, waits for them, and re-layouts  2.94 us
    ppermute x1, starting transfers between devices, on_device(): beside = lax.ppermute(block, ('gz', 'xy'), hop)  2.17 us
    pallas_call x1, Pallas kernels, on_device(): pl.pallas_call(relax_kernel, out_shape=shape, in_specs=[vmem, vmem], out_...  0.95 us
    ppermute x1, waiting for transfers between devices, on_device(): beside = lax.ppermute(block, ('gz', 'xy'), hop)  0.8 us
    ppermute x1, starting transfers between devices, on_device(): sent = lax.ppermute(peak_offsets, ('gz', 'xy'), fetch)  0.79 us
    pallas_call x1, Pallas kernels, on_device(): pl.pallas_call(flow_kernel, out_shape=shape, in_specs=[vmem], out_specs=v...  0.7 us
  transfers between devices with their start and end apart: 3, of which 1 were waited for; matrix products, arithmetic and copies ran while one was open for 0% of the time, Pallas kernels for 5%

profile of v7, /device:TPU:1, one launch (start us, length us, event | category | flops | bytes accessed | tf_op | source)
XLA Modules:
  0.0 27.5 jit_solution(4220511802546851331)
XLA Ops:
  0.6 3.3 %collective-permute-start.1 = (bf16[1,128,1024]{2,1,0:T(8,128)(2,1)}, bf16[1,128,1024]{2,1,0:T(8,128)(2,1)S(1)}, u32[]{:S(2)}, u32[]{:S(2)}) collective-permute-start(bf16[1,128,1024]{2,1,0:T(8,128)(2,1)} %own_ref.1), channel_id=1, source_target_pairs={{0,64},{1,0},{2,66},{3,2},{4,68},{5,4},{6,70},{7,6},{8,72},{9,8},{... | collective-permute-start | bytes 786440 | tf_op jit(solution)/shard_map/ppermute | solution.py:174
  3.9 0.8 %collective-permute-start = (s32[2,1,1,8]{3,2,1,0:T(1,128)}, s32[2,1,1,8]{3,2,1,0:T(1,128)S(1)}, u32[]{:S(2)}, u32[]{:S(2)}) collective-permute-start(s32[2,1,1,8]{3,2,1,0:T(1,128)} %peak_ref.1), channel_id=1, source_target_pairs={{0,2},{1,193},{2,0},{3,195},{4,6},{5,197},{6,4},{7,199},{8,10},{9,... | collective-permute-start | bytes 200 | tf_op jit(solution)/shard_map/ppermute | solution.py:175
  4.7 0.0 copy-start
  4.7 0.9 %copy-done = bf16[1,128,1024]{2,1,0:T(8,128)(2,1)S(1)} copy-done((bf16[1,128,1024]{2,1,0:T(8,128)(2,1)S(1)}, bf16[1,128,1024]{2,1,0:T(8,128)(2,1)}, u32[]{:S(2)}) %copy-start) | copy-done | bytes 262168
  5.6 0.0 copy-start.1
  5.6 0.7 %copy-done.1 = s32[2,1,1,8]{3,2,1,0:T(1,128)S(1)} copy-done((s32[2,1,1,8]{3,2,1,0:T(1,128)S(1)}, s32[2,1,1,8]{3,2,1,0:T(1,128)}, u32[]{:S(2)}) %copy-start.1) | copy-done | bytes 88
  6.3 0.0 copy-start.2
  6.3 0.7 %copy-done.2 = s32[1,1,8]{2,1,0:T(1,128)S(1)} copy-done((s32[1,1,8]{2,1,0:T(1,128)S(1)}, s32[1,1,8]{2,1,0:T(1,128)}, u32[]{:S(2)}) %copy-start.2) | copy-done | bytes 56
  7.0 0.0 copy-start.3
  7.0 0.7 %copy-done.3 = s32[1,1,8]{2,1,0:T(1,128)S(1)} copy-done((s32[1,1,8]{2,1,0:T(1,128)S(1)}, s32[1,1,8]{2,1,0:T(1,128)}, u32[]{:S(2)}) %copy-start.3) | copy-done | bytes 56
  7.6 0.5 %shard_map.59 = (f32[7,8,144,128]{3,2,1,0:T(8,128)S(1)}, f32[1,128]{1,0:T(1,128)S(1)}, s32[2,1,1,8]{3,2,1,0:T(1,128)S(1)}) custom-call(bf16[1,128,1024]{2,1,0:T(8,128)(2,1)S(1)} %copy-done, s32[2,1,1,8]{3,2,1,0:T(1,128)S(1)} %copy-done.1, s32[1,1,8]{2,1,0:T(1,128)S(1)} %copy-done.2, s32[1,1,8]{2,1,0:T(1,128)S(1)} %copy-done.3), custom_call_target="tpu_custom_call" | custom-call | tf_op jit(solution)/shard_map/pallas_call | solution.py:177
  8.1 0.0 collective-permute-done.sent_ref
  8.1 0.3 shard_map.60
  8.4 0.0 collective-permute-done.1.got_ref
  8.4 0.4 %shard_map.61 = f32[32,1,128]{2,1,0:T(1,128)S(1)} custom-call(f32[5,8,128,128]{3,2,1,0:T(8,128)S(1)} %get-tuple-element.10.windows_ref, bf16[1,128,1024]{2,1,0:T(8,128)(2,1)S(1)} %collective-permute-done.1.got_ref, f32[1,128]{1,0:T(1,128)S(1)} %get-tuple-element.11.fixed_ref), custom_call_target="tpu_custom_call" | custom-call | tf_op jit(solution)/shard_map/pallas_call | solution.py:198
  8.8 14.1 %all_to_all.5 = f32[32,1,128]{2,1,0:T(1,128)S(1)} all-to-all(f32[32,1,128]{2,1,0:T(1,128)S(1)} %shard_map.61), channel_id=1, replica_groups={{0,1,2,3,4,5,6,7,64,65,66,67,68,69,70,71,128,129,130,131,132,133,134,13..., dimensions={0} | all-to-all | bytes 32768 | tf_op jit(solution)/shard_map/all_to_all | solution.py:209
  22.9 2.2 %collective-permute-start.2 = (f32[8,128]{1,0:T(8,128)S(1)}, f32[8,128]{1,0:T(8,128)S(1)}, u32[]{:S(2)}, u32[]{:S(2)}) collective-permute-start(f32[8,128]{1,0:T(8,128)S(1)} %bitcast_reduce_fusion.own_ref), channel_id=1, source_target_pairs={{0,9},{1,8},{2,11},{3,10},{4,2},{5,3},{6,0},{7,1},{8,17},{9,16},{1... | collective-permute-start | bytes 12296 | tf_op jit(solution)/shard_map/ppermute | solution.py:211
  25.1 0.7 %shard_map.62 = f32[2,1,1,8]{3,2,1,0:T(1,128)} custom-call(f32[8,128]{1,0:T(8,128)S(1)} %bitcast_reduce_fusion.own_ref), custom_call_target="tpu_custom_call" | custom-call | tf_op jit(solution)/shard_map/pallas_call | solution.py:213
  25.8 0.8 %collective-permute-done.2.got_ref = f32[8,128]{1,0:T(8,128)S(1)} collective-permute-done((f32[8,128]{1,0:T(8,128)S(1)}, f32[8,128]{1,0:T(8,128)S(1)}, u32[]{:S(2)}, u32[]{:S(2)}) %collective-permute-start.2) | collective-permute-done | bytes 4128 | tf_op jit(solution)/shard_map/ppermute | solution.py:211
  26.6 0.9 %shard_map.63 = f32[2,1,1,8]{3,2,1,0:T(1,128)} custom-call(f32[8,128]{1,0:T(8,128)S(1)} %bitcast_reduce_fusion.own_ref, f32[8,128]{1,0:T(8,128)S(1)} %collective-permute-done.2.got_ref), custom_call_target="tpu_custom_call" | custom-call | tf_op jit(solution)/shard_map/pallas_call | solution.py:220
  (1 shorter events, 0.0 us)
Async XLA Ops:
  0.6 7.8 %collective-permute-start.1 = (bf16[1,128,1024]{2,1,0:T(8,128)(2,1)}, bf16[1,128,1024]{2,1,0:T(8,128)(2,1)S(1)}, u32[]{:S(2)}, u32[]{:S(2)}) collective-permute-start(bf16[1,128,1024]{2,1,0:T(8,128)(2,1)} %own_ref.1), channel_id=1, source_target_pairs={{0,64},{1,0},{2,66},{3,2},{4,68},{5,4},{6,70},{7,6},{8,72},{9,8},{... | collective-permute-start | bytes 786440 | tf_op jit(solution)/shard_map/ppermute | solution.py:174
  3.9 4.2 %collective-permute-start = (s32[2,1,1,8]{3,2,1,0:T(1,128)}, s32[2,1,1,8]{3,2,1,0:T(1,128)S(1)}, u32[]{:S(2)}, u32[]{:S(2)}) collective-permute-start(s32[2,1,1,8]{3,2,1,0:T(1,128)} %peak_ref.1), channel_id=1, source_target_pairs={{0,2},{1,193},{2,0},{3,195},{4,6},{5,197},{6,4},{7,199},{8,10},{9,... | collective-permute-start | bytes 200 | tf_op jit(solution)/shard_map/ppermute | solution.py:175
  4.7 0.9 %copy-start = (bf16[1,128,1024]{2,1,0:T(8,128)(2,1)S(1)}, bf16[1,128,1024]{2,1,0:T(8,128)(2,1)}, u32[]{:S(2)}) copy-start(bf16[1,128,1024]{2,1,0:T(8,128)(2,1)} %own_ref.1) | copy-start | bytes 786436
  5.6 0.7 %copy-start.1 = (s32[2,1,1,8]{3,2,1,0:T(1,128)S(1)}, s32[2,1,1,8]{3,2,1,0:T(1,128)}, u32[]{:S(2)}) copy-start(s32[2,1,1,8]{3,2,1,0:T(1,128)} %peak_ref.1) | copy-start | bytes 196
  6.3 0.7 %copy-start.2 = (s32[1,1,8]{2,1,0:T(1,128)S(1)}, s32[1,1,8]{2,1,0:T(1,128)}, u32[]{:S(2)}) copy-start(s32[1,1,8]{2,1,0:T(1,128)} %conf_ref.1) | copy-start | bytes 100
  7.0 0.7 %copy-start.3 = (s32[1,1,8]{2,1,0:T(1,128)S(1)}, s32[1,1,8]{2,1,0:T(1,128)}, u32[]{:S(2)}) copy-start(s32[1,1,8]{2,1,0:T(1,128)} %mask_ref.1) | copy-start | bytes 100
  22.9 3.7 %collective-permute-start.2 = (f32[8,128]{1,0:T(8,128)S(1)}, f32[8,128]{1,0:T(8,128)S(1)}, u32[]{:S(2)}, u32[]{:S(2)}) collective-permute-start(f32[8,128]{1,0:T(8,128)S(1)} %bitcast_reduce_fusion.own_ref), channel_id=1, source_target_pairs={{0,9},{1,8},{2,11},{3,10},{4,2},{5,3},{6,0},{7,1},{8,17},{9,16},{1... | collective-permute-start | bytes 12296 | tf_op jit(solution)/shard_map/ppermute | solution.py:211

commit v8 on v5

--- a/solution.py
+++ b/solution.py
@@ -102,7 +102,6 @@
     got = got_ref[...]
     window = jnp.concatenate([jnp.where(upper, got, own), jnp.where(upper, own, got)], axis=0)
     base = jnp.where(upper, z - 1, z) * PLANE
-    here = jnp.where(upper, PLANE + inner, inner)
     shape = (2 * PLANE, LANES)
     lane = lax.broadcasted_iota(jnp.int32, shape, 1)
     local = lax.broadcasted_iota(jnp.int32, shape, 0)
@@ -130,12 +129,11 @@
         links = stiff * (pltpu.roll(moved, 16, 1) - moved)
         links = links + next_stiff * (pltpu.roll(moved, LANES - 16, 1) - moved)
         moved = (moved + first) + (neighbours(moved) + links)
-    turn = lax.rem(LANES - gz * 16, LANES)
     for value, ref in ((flow, flow_ref), (moved, corr_ref)):
-        mine = jnp.sum(jnp.where(local == here, value, 0.0), axis=0, keepdims=True)
-        mine = pltpu.roll(mine, turn, 1)
-        ref[0, 0] = mine[:, 0:COLS]
-        ref[1, 0] = mine[:, COLS : 2 * COLS]
+        mine = jnp.where(upper, value[PLANE:], value[:PLANE])
+        mine = pltpu.roll(mine, lax.rem(PLANE - inner, PLANE), 0)[0:1]
+        ref[0, 0] = pltpu.roll(mine, lax.rem(LANES - gz * 16, LANES), 1)[:, 0:COLS]
+        ref[1, 0] = pltpu.roll(mine, LANES - COLS - gz * 16, 1)[:, 0:COLS]
 
 
 def routes(groups, strips):

time: 27.8 us -> 27.7 us (level)
  no operation moved by 1% of the time
where the time goes in v8:
time: 27.7 us; the launch traced here: 27.5 us
  blocking collectives  14.1 us (51%)
  starting transfers between devices  6.21 us (22%)
  local copies, waits for them, and re-layouts  2.94 us (11%)
  Pallas kernels  2.08 us (8%)
  waiting for transfers between devices  1.5 us (5%)
  between operations  0.66 us (2%)
    all_to_all x1, blocking collectives, on_device(): lax.all_to_all(row, ('gz', 'xy'), 0, 0, axis_index_groups=planes, tiled=T...  14.1 us
    ppermute x1, starting transfers between devices, on_device(): got = lax.ppermute(sections, ('gz', 'xy'), swap)  3.26 us
    unnamed x8, local copies, waits for them, and re-layouts  2.94 us
    ppermute x1, starting transfers between devices, on_device(): beside = lax.ppermute(block, ('gz', 'xy'), hop)  2.17 us
    ppermute x1, waiting for transfers between devices, on_device(): beside = lax.ppermute(block, ('gz', 'xy'), hop)  1.5 us
    pallas_call x1, Pallas kernels, on_device(): pl.pallas_call(relax_kernel, out_shape=(shape, shape), in_specs=[vmem, vm...  0.95 us
    ppermute x1, starting transfers between devices, on_device(): sent = lax.ppermute(peak_offsets, ('gz', 'xy'), fetch)  0.79 us
  transfers between devices with their start and end apart: 3, of which 1 were waited for; matrix products, arithmetic and copies ran while one was open for 0% of the time, Pallas kernels for 3%

profile of v8, /device:TPU:1, one launch (start us, length us, event | category | flops | bytes accessed | tf_op | source)
XLA Modules:
  0.0 27.5 jit_solution(18289322103837842067)
XLA Ops:
  0.6 3.3 %collective-permute-start.1 = (bf16[1,128,1024]{2,1,0:T(8,128)(2,1)}, bf16[1,128,1024]{2,1,0:T(8,128)(2,1)S(1)}, u32[]{:S(2)}, u32[]{:S(2)}) collective-permute-start(bf16[1,128,1024]{2,1,0:T(8,128)(2,1)} %own_ref.1), channel_id=1, source_target_pairs={{0,64},{1,0},{2,66},{3,2},{4,68},{5,4},{6,70},{7,6},{8,72},{9,8},{... | collective-permute-start | bytes 786440 | tf_op jit(solution)/shard_map/ppermute | solution.py:165
  3.9 0.8 %collective-permute-start = (s32[2,1,1,8]{3,2,1,0:T(1,128)}, s32[2,1,1,8]{3,2,1,0:T(1,128)S(1)}, u32[]{:S(2)}, u32[]{:S(2)}) collective-permute-start(s32[2,1,1,8]{3,2,1,0:T(1,128)} %peak_ref.1), channel_id=1, source_target_pairs={{0,2},{1,193},{2,0},{3,195},{4,6},{5,197},{6,4},{7,199},{8,10},{9,... | collective-permute-start | bytes 200 | tf_op jit(solution)/shard_map/ppermute | solution.py:166
  4.7 0.0 copy-start
  4.7 0.9 %copy-done = bf16[1,128,1024]{2,1,0:T(8,128)(2,1)S(1)} copy-done((bf16[1,128,1024]{2,1,0:T(8,128)(2,1)S(1)}, bf16[1,128,1024]{2,1,0:T(8,128)(2,1)}, u32[]{:S(2)}) %copy-start) | copy-done | bytes 262168
  5.6 0.0 copy-start.1
  5.6 0.7 %copy-done.1 = s32[2,1,1,8]{3,2,1,0:T(1,128)S(1)} copy-done((s32[2,1,1,8]{3,2,1,0:T(1,128)S(1)}, s32[2,1,1,8]{3,2,1,0:T(1,128)}, u32[]{:S(2)}) %copy-start.1) | copy-done | bytes 88
  6.3 0.0 copy-start.2
  6.3 0.7 %copy-done.2 = s32[1,1,8]{2,1,0:T(1,128)S(1)} copy-done((s32[1,1,8]{2,1,0:T(1,128)S(1)}, s32[1,1,8]{2,1,0:T(1,128)}, u32[]{:S(2)}) %copy-start.2) | copy-done | bytes 56
  7.0 0.0 copy-start.3
  7.0 0.7 %copy-done.3 = s32[1,1,8]{2,1,0:T(1,128)S(1)} copy-done((s32[1,1,8]{2,1,0:T(1,128)S(1)}, s32[1,1,8]{2,1,0:T(1,128)}, u32[]{:S(2)}) %copy-start.3) | copy-done | bytes 56
  7.6 0.5 %shard_map.59 = (f32[7,8,144,128]{3,2,1,0:T(8,128)S(1)}, f32[1,128]{1,0:T(1,128)S(1)}, s32[2,1,1,8]{3,2,1,0:T(1,128)S(1)}) custom-call(bf16[1,128,1024]{2,1,0:T(8,128)(2,1)S(1)} %copy-done, s32[2,1,1,8]{3,2,1,0:T(1,128)S(1)} %copy-done.1, s32[1,1,8]{2,1,0:T(1,128)S(1)} %copy-done.2, s32[1,1,8]{2,1,0:T(1,128)S(1)} %copy-done.3), custom_call_target="tpu_custom_call" | custom-call | tf_op jit(solution)/shard_map/pallas_call | solution.py:168
  8.1 0.0 collective-permute-done.sent_ref
  8.1 0.3 shard_map.60
  8.4 0.0 collective-permute-done.1.got_ref
  8.4 0.4 %shard_map.61 = f32[32,1,128]{2,1,0:T(1,128)S(1)} custom-call(f32[5,8,128,128]{3,2,1,0:T(8,128)S(1)} %get-tuple-element.10.windows_ref, bf16[1,128,1024]{2,1,0:T(8,128)(2,1)S(1)} %collective-permute-done.1.got_ref, f32[1,128]{1,0:T(1,128)S(1)} %get-tuple-element.11.fixed_ref), custom_call_target="tpu_custom_call" | custom-call | tf_op jit(solution)/shard_map/pallas_call | solution.py:189
  8.8 14.1 %all_to_all.5 = f32[32,1,128]{2,1,0:T(1,128)S(1)} all-to-all(f32[32,1,128]{2,1,0:T(1,128)S(1)} %shard_map.61), channel_id=1, replica_groups={{0,1,2,3,4,5,6,7,64,65,66,67,68,69,70,71,128,129,130,131,132,133,134,13..., dimensions={0} | all-to-all | bytes 32768 | tf_op jit(solution)/shard_map/all_to_all | solution.py:200
  22.9 2.2 %collective-permute-start.2 = (f32[8,128]{1,0:T(8,128)S(1)}, f32[8,128]{1,0:T(8,128)S(1)}, u32[]{:S(2)}, u32[]{:S(2)}) collective-permute-start(f32[8,128]{1,0:T(8,128)S(1)} %bitcast_reduce_fusion.own_ref), channel_id=1, source_target_pairs={{0,9},{1,8},{2,11},{3,10},{4,2},{5,3},{6,0},{7,1},{8,17},{9,16},{1... | collective-permute-start | bytes 12296 | tf_op jit(solution)/shard_map/ppermute | solution.py:202
  25.1 1.5 %collective-permute-done.2.got_ref = f32[8,128]{1,0:T(8,128)S(1)} collective-permute-done((f32[8,128]{1,0:T(8,128)S(1)}, f32[8,128]{1,0:T(8,128)S(1)}, u32[]{:S(2)}, u32[]{:S(2)}) %collective-permute-start.2) | collective-permute-done | bytes 4128 | tf_op jit(solution)/shard_map/ppermute | solution.py:202
  26.6 1.0 %shard_map.62 = (f32[2,1,1,8]{3,2,1,0:T(1,128)}, f32[2,1,1,8]{3,2,1,0:T(1,128)}) custom-call(f32[8,128]{1,0:T(8,128)S(1)} %bitcast_reduce_fusion.own_ref, f32[8,128]{1,0:T(8,128)S(1)} %collective-permute-done.2.got_ref), custom_call_target="tpu_custom_call" | custom-call | tf_op jit(solution)/shard_map/pallas_call | solution.py:204
  (1 shorter events, 0.0 us)
Async XLA Ops:
  0.6 7.8 %collective-permute-start.1 = (bf16[1,128,1024]{2,1,0:T(8,128)(2,1)}, bf16[1,128,1024]{2,1,0:T(8,128)(2,1)S(1)}, u32[]{:S(2)}, u32[]{:S(2)}) collective-permute-start(bf16[1,128,1024]{2,1,0:T(8,128)(2,1)} %own_ref.1), channel_id=1, source_target_pairs={{0,64},{1,0},{2,66},{3,2},{4,68},{5,4},{6,70},{7,6},{8,72},{9,8},{... | collective-permute-start | bytes 786440 | tf_op jit(solution)/shard_map/ppermute | solution.py:165
  3.9 4.2 %collective-permute-start = (s32[2,1,1,8]{3,2,1,0:T(1,128)}, s32[2,1,1,8]{3,2,1,0:T(1,128)S(1)}, u32[]{:S(2)}, u32[]{:S(2)}) collective-permute-start(s32[2,1,1,8]{3,2,1,0:T(1,128)} %peak_ref.1), channel_id=1, source_target_pairs={{0,2},{1,193},{2,0},{3,195},{4,6},{5,197},{6,4},{7,199},{8,10},{9,... | collective-permute-start | bytes 200 | tf_op jit(solution)/shard_map/ppermute | solution.py:166
  4.7 0.9 %copy-start = (bf16[1,128,1024]{2,1,0:T(8,128)(2,1)S(1)}, bf16[1,128,1024]{2,1,0:T(8,128)(2,1)}, u32[]{:S(2)}) copy-start(bf16[1,128,1024]{2,1,0:T(8,128)(2,1)} %own_ref.1) | copy-start | bytes 786436
  5.6 0.7 %copy-start.1 = (s32[2,1,1,8]{3,2,1,0:T(1,128)S(1)}, s32[2,1,1,8]{3,2,1,0:T(1,128)}, u32[]{:S(2)}) copy-start(s32[2,1,1,8]{3,2,1,0:T(1,128)} %peak_ref.1) | copy-start | bytes 196
  6.3 0.7 %copy-start.2 = (s32[1,1,8]{2,1,0:T(1,128)S(1)}, s32[1,1,8]{2,1,0:T(1,128)}, u32[]{:S(2)}) copy-start(s32[1,1,8]{2,1,0:T(1,128)} %conf_ref.1) | copy-start | bytes 100
  7.0 0.7 %copy-start.3 = (s32[1,1,8]{2,1,0:T(1,128)S(1)}, s32[1,1,8]{2,1,0:T(1,128)}, u32[]{:S(2)}) copy-start(s32[1,1,8]{2,1,0:T(1,128)} %mask_ref.1) | copy-start | bytes 100
  22.9 3.7 %collective-permute-start.2 = (f32[8,128]{1,0:T(8,128)S(1)}, f32[8,128]{1,0:T(8,128)S(1)}, u32[]{:S(2)}, u32[]{:S(2)}) collective-permute-start(f32[8,128]{1,0:T(8,128)S(1)} %bitcast_reduce_fusion.own_ref), channel_id=1, source_target_pairs={{0,9},{1,8},{2,11},{3,10},{4,2},{5,3},{6,0},{7,1},{8,17},{9,16},{1... | collective-permute-start | bytes 12296 | tf_op jit(solution)/shard_map/ppermute | solution.py:202

commit v9 on v5

--- a/solution.py
+++ b/solution.py
@@ -126,10 +126,13 @@
 
     first = neighbours(start)
     moved = first
+    sides = [jnp.where(has, STEP_SIZE, 0.0) for has in (has_up, has_down, has_left, has_right)]
+    keep = 1.0 - ((sides[0] + sides[1]) + (sides[2] + sides[3]) + (stiff + next_stiff))
     for _ in range(ITERS - 1):
-        links = stiff * (pltpu.roll(moved, 16, 1) - moved)
-        links = links + next_stiff * (pltpu.roll(moved, LANES - 16, 1) - moved)
-        moved = (moved + first) + (neighbours(moved) + links)
+        rows = sides[0] * pltpu.roll(moved, 1, 0) + sides[1] * pltpu.roll(moved, 2 * PLANE - 1, 0)
+        cols = sides[2] * pltpu.roll(moved, 1, 1) + sides[3] * pltpu.roll(moved, LANES - 1, 1)
+        links = stiff * pltpu.roll(moved, 16, 1) + next_stiff * pltpu.roll(moved, LANES - 16, 1)
+        moved = (keep * moved + first) + ((rows + cols) + links)
     turn = lax.rem(LANES - gz * 16, LANES)
     for value, ref in ((flow, flow_ref), (moved, corr_ref)):
         mine = jnp.sum(jnp.where(local == here, value, 0.0), axis=0, keepdims=True)

time: 27.8 us -> 27.8 us (level)
  no operation moved by 1% of the time
where the time goes in v9:
time: 27.8 us; the launch traced here: 27.6 us
  blocking collectives  14.1 us (51%)
  starting transfers between devices  6.21 us (22%)
  local copies, waits for them, and re-layouts  2.94 us (11%)
  Pallas kernels  2.15 us (8%)
  waiting for transfers between devices  1.5 us (5%)
  between operations  0.66 us (2%)
    all_to_all x1, blocking collectives, on_device(): lax.all_to_all(row, ('gz', 'xy'), 0, 0, axis_index_groups=planes, tiled=T...  14.1 us
    ppermute x1, starting transfers between devices, on_device(): got = lax.ppermute(sections, ('gz', 'xy'), swap)  3.26 us
    unnamed x8, local copies, waits for them, and re-layouts  2.94 us
    ppermute x1, starting transfers between devices, on_device(): beside = lax.ppermute(block, ('gz', 'xy'), hop)  2.17 us
    ppermute x1, waiting for transfers between devices, on_device(): beside = lax.ppermute(block, ('gz', 'xy'), hop)  1.5 us
    pallas_call x1, Pallas kernels, on_device(): pl.pallas_call(relax_kernel, out_shape=(shape, shape), in_specs=[vmem, vm...  1.02 us
    ppermute x1, starting transfers between devices, on_device(): sent = lax.ppermute(peak_offsets, ('gz', 'xy'), fetch)  0.79 us
  transfers between devices with their start and end apart: 3, of which 1 were waited for; matrix products, arithmetic and copies ran while one was open for 0% of the time, Pallas kernels for 3%

profile of v9, /device:TPU:1, one launch (start us, length us, event | category | flops | bytes accessed | tf_op | source)
XLA Modules:
  0.0 27.6 jit_solution(5188506031958743945)
XLA Ops:
  0.6 3.3 %collective-permute-start.1 = (bf16[1,128,1024]{2,1,0:T(8,128)(2,1)}, bf16[1,128,1024]{2,1,0:T(8,128)(2,1)S(1)}, u32[]{:S(2)}, u32[]{:S(2)}) collective-permute-start(bf16[1,128,1024]{2,1,0:T(8,128)(2,1)} %own_ref.1), channel_id=1, source_target_pairs={{0,64},{1,0},{2,66},{3,2},{4,68},{5,4},{6,70},{7,6},{8,72},{9,8},{... | collective-permute-start | bytes 786440 | tf_op jit(solution)/shard_map/ppermute | solution.py:170
  3.9 0.8 %collective-permute-start = (s32[2,1,1,8]{3,2,1,0:T(1,128)}, s32[2,1,1,8]{3,2,1,0:T(1,128)S(1)}, u32[]{:S(2)}, u32[]{:S(2)}) collective-permute-start(s32[2,1,1,8]{3,2,1,0:T(1,128)} %peak_ref.1), channel_id=1, source_target_pairs={{0,2},{1,193},{2,0},{3,195},{4,6},{5,197},{6,4},{7,199},{8,10},{9,... | collective-permute-start | bytes 200 | tf_op jit(solution)/shard_map/ppermute | solution.py:171
  4.7 0.0 copy-start
  4.7 0.9 %copy-done = bf16[1,128,1024]{2,1,0:T(8,128)(2,1)S(1)} copy-done((bf16[1,128,1024]{2,1,0:T(8,128)(2,1)S(1)}, bf16[1,128,1024]{2,1,0:T(8,128)(2,1)}, u32[]{:S(2)}) %copy-start) | copy-done | bytes 262168
  5.6 0.0 copy-start.1
  5.6 0.7 %copy-done.1 = s32[2,1,1,8]{3,2,1,0:T(1,128)S(1)} copy-done((s32[2,1,1,8]{3,2,1,0:T(1,128)S(1)}, s32[2,1,1,8]{3,2,1,0:T(1,128)}, u32[]{:S(2)}) %copy-start.1) | copy-done | bytes 88
  6.3 0.0 copy-start.2
  6.3 0.7 %copy-done.2 = s32[1,1,8]{2,1,0:T(1,128)S(1)} copy-done((s32[1,1,8]{2,1,0:T(1,128)S(1)}, s32[1,1,8]{2,1,0:T(1,128)}, u32[]{:S(2)}) %copy-start.2) | copy-done | bytes 56
  7.0 0.0 copy-start.3
  7.0 0.7 %copy-done.3 = s32[1,1,8]{2,1,0:T(1,128)S(1)} copy-done((s32[1,1,8]{2,1,0:T(1,128)S(1)}, s32[1,1,8]{2,1,0:T(1,128)}, u32[]{:S(2)}) %copy-start.3) | copy-done | bytes 56
  7.6 0.5 %shard_map.59 = (f32[7,8,144,128]{3,2,1,0:T(8,128)S(1)}, f32[1,128]{1,0:T(1,128)S(1)}, s32[2,1,1,8]{3,2,1,0:T(1,128)S(1)}) custom-call(bf16[1,128,1024]{2,1,0:T(8,128)(2,1)S(1)} %copy-done, s32[2,1,1,8]{3,2,1,0:T(1,128)S(1)} %copy-done.1, s32[1,1,8]{2,1,0:T(1,128)S(1)} %copy-done.2, s32[1,1,8]{2,1,0:T(1,128)S(1)} %copy-done.3), custom_call_target="tpu_custom_call" | custom-call | tf_op jit(solution)/shard_map/pallas_call | solution.py:173
  8.1 0.0 collective-permute-done.sent_ref
  8.1 0.3 shard_map.60
  8.4 0.0 collective-permute-done.1.got_ref
  8.4 0.4 %shard_map.61 = f32[32,1,128]{2,1,0:T(1,128)S(1)} custom-call(f32[5,8,128,128]{3,2,1,0:T(8,128)S(1)} %get-tuple-element.10.windows_ref, bf16[1,128,1024]{2,1,0:T(8,128)(2,1)S(1)} %collective-permute-done.1.got_ref, f32[1,128]{1,0:T(1,128)S(1)} %get-tuple-element.11.fixed_ref), custom_call_target="tpu_custom_call" | custom-call | tf_op jit(solution)/shard_map/pallas_call | solution.py:194
  8.8 14.1 %all_to_all.5 = f32[32,1,128]{2,1,0:T(1,128)S(1)} all-to-all(f32[32,1,128]{2,1,0:T(1,128)S(1)} %shard_map.61), channel_id=1, replica_groups={{0,1,2,3,4,5,6,7,64,65,66,67,68,69,70,71,128,129,130,131,132,133,134,13..., dimensions={0} | all-to-all | bytes 32768 | tf_op jit(solution)/shard_map/all_to_all | solution.py:205
  22.9 2.2 %collective-permute-start.2 = (f32[8,128]{1,0:T(8,128)S(1)}, f32[8,128]{1,0:T(8,128)S(1)}, u32[]{:S(2)}, u32[]{:S(2)}) collective-permute-start(f32[8,128]{1,0:T(8,128)S(1)} %bitcast_reduce_fusion.own_ref), channel_id=1, source_target_pairs={{0,9},{1,8},{2,11},{3,10},{4,2},{5,3},{6,0},{7,1},{8,17},{9,16},{1... | collective-permute-start | bytes 12296 | tf_op jit(solution)/shard_map/ppermute | solution.py:207
  25.1 1.5 %collective-permute-done.2.got_ref = f32[8,128]{1,0:T(8,128)S(1)} collective-permute-done((f32[8,128]{1,0:T(8,128)S(1)}, f32[8,128]{1,0:T(8,128)S(1)}, u32[]{:S(2)}, u32[]{:S(2)}) %collective-permute-start.2) | collective-permute-done | bytes 4128 | tf_op jit(solution)/shard_map/ppermute | solution.py:207
  26.6 1.0 %shard_map.62 = (f32[2,1,1,8]{3,2,1,0:T(1,128)}, f32[2,1,1,8]{3,2,1,0:T(1,128)}) custom-call(f32[8,128]{1,0:T(8,128)S(1)} %bitcast_reduce_fusion.own_ref, f32[8,128]{1,0:T(8,128)S(1)} %collective-permute-done.2.got_ref), custom_call_target="tpu_custom_call" | custom-call | tf_op jit(solution)/shard_map/pallas_call | solution.py:209
  (1 shorter events, 0.0 us)
Async XLA Ops:
  0.6 7.8 %collective-permute-start.1 = (bf16[1,128,1024]{2,1,0:T(8,128)(2,1)}, bf16[1,128,1024]{2,1,0:T(8,128)(2,1)S(1)}, u32[]{:S(2)}, u32[]{:S(2)}) collective-permute-start(bf16[1,128,1024]{2,1,0:T(8,128)(2,1)} %own_ref.1), channel_id=1, source_target_pairs={{0,64},{1,0},{2,66},{3,2},{4,68},{5,4},{6,70},{7,6},{8,72},{9,8},{... | collective-permute-start | bytes 786440 | tf_op jit(solution)/shard_map/ppermute | solution.py:170
  3.9 4.2 %collective-permute-start = (s32[2,1,1,8]{3,2,1,0:T(1,128)}, s32[2,1,1,8]{3,2,1,0:T(1,128)S(1)}, u32[]{:S(2)}, u32[]{:S(2)}) collective-permute-start(s32[2,1,1,8]{3,2,1,0:T(1,128)} %peak_ref.1), channel_id=1, source_target_pairs={{0,2},{1,193},{2,0},{3,195},{4,6},{5,197},{6,4},{7,199},{8,10},{9,... | collective-permute-start | bytes 200 | tf_op jit(solution)/shard_map/ppermute | solution.py:171
  4.7 0.9 %copy-start = (bf16[1,128,1024]{2,1,0:T(8,128)(2,1)S(1)}, bf16[1,128,1024]{2,1,0:T(8,128)(2,1)}, u32[]{:S(2)}) copy-start(bf16[1,128,1024]{2,1,0:T(8,128)(2,1)} %own_ref.1) | copy-start | bytes 786436
  5.6 0.7 %copy-start.1 = (s32[2,1,1,8]{3,2,1,0:T(1,128)S(1)}, s32[2,1,1,8]{3,2,1,0:T(1,128)}, u32[]{:S(2)}) copy-start(s32[2,1,1,8]{3,2,1,0:T(1,128)} %peak_ref.1) | copy-start | bytes 196
  6.3 0.7 %copy-start.2 = (s32[1,1,8]{2,1,0:T(1,128)S(1)}, s32[1,1,8]{2,1,0:T(1,128)}, u32[]{:S(2)}) copy-start(s32[1,1,8]{2,1,0:T(1,128)} %conf_ref.1) | copy-start | bytes 100
  7.0 0.7 %copy-start.3 = (s32[1,1,8]{2,1,0:T(1,128)S(1)}, s32[1,1,8]{2,1,0:T(1,128)}, u32[]{:S(2)}) copy-start(s32[1,1,8]{2,1,0:T(1,128)} %mask_ref.1) | copy-start | bytes 100
  22.9 3.7 %collective-permute-start.2 = (f32[8,128]{1,0:T(8,128)S(1)}, f32[8,128]{1,0:T(8,128)S(1)}, u32[]{:S(2)}, u32[]{:S(2)}) collective-permute-start(f32[8,128]{1,0:T(8,128)S(1)} %bitcast_reduce_fusion.own_ref), channel_id=1, source_target_pairs={{0,9},{1,8},{2,11},{3,10},{4,2},{5,3},{6,0},{7,1},{8,17},{9,16},{1... | collective-permute-start | bytes 12296 | tf_op jit(solution)/shard_map/ppermute | solution.py:207
